TPU v7x, 128 devices: a whole 4x4x4 slice. The times are simulated.
128 devices in a mesh: row: 8 (over y, core), col: 16 (over x, z).
Axes of the slice: x: 4, y: 4, z: 4, core: 2. Of those that a mesh axis runs over, the one named last changes fastest.
Arguments:
- hidden_in: bfloat16 [256, 2, 6144], P(('row', 'col')), may hold values from -6 to 6
- queries: bfloat16 [256, 2, 6144], P(('row', 'col')), may hold values from -9 to 9
- new_kv: bfloat16 [256, 2, 2048], P(('row', 'col')), may hold values from -6 to 6
- kv_pool: bfloat16 [4096, 16, 2048], P(('row', 'col')), may hold values from -6 to 6
- block_table: int32 [256, 64], replicated, may hold values from -1 to 4095, as said below
- cached_len: int32 [256], replicated, may hold values from 1 to 1024, as said below
- w_out: bfloat16 [6144, 6144], P('col'), may hold values from -0.078125 to 0.078125
- norm_gain: bfloat16 [6144], replicated, may hold values from 0.5 to 1.5
- expert_ids: int32 [256, 2, 2], P(('row', 'col')), may hold values from 0 to 7, all different within a row; in each aligned block of 4 rows (0 to 3, 4 to 7, ..., all dimensions but the last counted through in order) at most 3 rows name the same one
- expert_gates: float32 [256, 2, 2], P(('row', 'col')), may hold values from 0.2 to 1
- w_gate: bfloat16 [8, 6144, 8192], P('row', None, 'col'), may hold values from -0.078125 to 0.078125
- w_up: bfloat16 [8, 6144, 8192], P('row', None, 'col'), may hold values from -0.078125 to 0.078125
- w_down: bfloat16 [8, 8192, 6144], P('row', 'col'), may hold values from -0.0625 to 0.0625
Outputs:
- layer_out: bfloat16 [256, 2, 6144], P(('row', 'col'))
Inputs may be any that keep to these rules, and one draw needn't show every extreme that they name: `block_table`: row i lists request i's blocks in order for b < ceil(cached_len[i] / 16) and -1 after; no block is listed twice; the blocks of device d are rows d * 32 to d * 32 + 31 of kv_pool; in every draw all 32 blocks of some device are listed. `cached_len`: some request has exactly 1024 cached positions. `expert_ids`: the two experts of a token-step differ; among the 4 token-steps of one device (aligned blocks of rows in request-major order) no expert is named more than 3 times.
All inputs are finite; a program needn't handle non-finite values.
Results may differ from a plain program's by a relative error of at most 0.018.
Values may be sent and summed in bfloat16 or wider, within the bound.
A program may use at most 192 MiB of HBM per device.

v0:
```python
import jax
import jax.numpy as jnp
from jax import lax
from jax.sharding import PartitionSpec as P

HEADS = 48
KVH = 8
HD = 128
EXPERTS = 8
TOPK = 2
CAP = 3


floor_score = -1e30


def on_device(
    hidden_in,
    queries,
    new_kv,
    kv_pool,
    block_table,
    cached_len,
    w_out,
    norm_gain,
    expert_ids,
    expert_gates,
    w_gate,
    w_up,
    w_down,
):
    req_local = hidden_in.shape[0]
    steps = hidden_in.shape[1]
    width = hidden_in.shape[2]
    groups = HEADS // KVH
    kv_width = KVH * HD
    heads_total = steps * HEADS
    scale = HD ** (-0.5)
    blocks_here = kv_pool.shape[0]
    block_size = kv_pool.shape[1]
    requests = block_table.shape[0]
    max_blocks = block_table.shape[1]
    device_rank = lax.axis_index(("row", "col"))
    slot_ids = device_rank * blocks_here + jnp.arange(blocks_here, dtype=jnp.int32)
    matches = block_table[None, :, :] == slot_ids[:, None, None]
    holder = jnp.any(matches, axis=2)
    holder_half = holder.astype(jnp.bfloat16)
    holder_single = holder.astype(jnp.float32)
    block_rank = jnp.sum(
        jnp.where(matches, jnp.arange(max_blocks, dtype=jnp.int32)[None, None, :], 0), axis=(1, 2)
    )
    slot_length = jnp.sum(jnp.where(holder, cached_len[None, :], 0), axis=1)
    positions = block_rank[:, None] * block_size + jnp.arange(block_size, dtype=jnp.int32)[None, :]
    visible = positions < slot_length[:, None]
    flat_queries = queries.reshape(req_local, steps * width)
    slot_queries = jnp.dot(
        holder_half,
        lax.all_gather(flat_queries, ("row", "col"), axis=0, tiled=True),
        preferred_element_type=jnp.float32,
    )
    query_blocks = slot_queries.astype(jnp.bfloat16).reshape(blocks_here, steps, KVH, groups, HD)
    keys_here = kv_pool[:, :, :kv_width].reshape(blocks_here, block_size, KVH, HD)
    values_here = (
        kv_pool[:, :, kv_width:].astype(jnp.float32).reshape(blocks_here, block_size, KVH, HD)
    )
    scores = (
        jnp.einsum("jskgd,jtkd->jskgt", query_blocks, keys_here, preferred_element_type=jnp.float32)
        * scale
    )
    scores = jnp.where(visible[:, None, None, None, :], scores, floor_score)
    slot_top = jnp.max(scores, axis=4).reshape(blocks_here, heads_total)
    request_top = jnp.max(jnp.where(holder[:, :, None], slot_top[:, None, :], floor_score), axis=0)
    back_top = jnp.sum(jnp.where(holder[:, :, None], request_top[None, :, :], 0.0), axis=1)
    weights = jnp.exp(scores - back_top.reshape(blocks_here, steps, KVH, groups)[..., None])
    slot_sums = jnp.sum(weights, axis=4).reshape(blocks_here, heads_total)
    slot_mixed = jnp.einsum(
        "jskgt,jtkd->jskgd", weights, values_here, precision=lax.Precision.HIGHEST
    )
    request_mixed = jnp.dot(
        holder_single.T,
        slot_mixed.reshape(blocks_here, steps * width),
        precision=lax.Precision.HIGHEST,
    )
    request_sums = jnp.dot(holder_single.T, slot_sums, precision=lax.Precision.HIGHEST)
    global_top = lax.pmax(request_top.astype(jnp.bfloat16), ("row", "col")).astype(
        request_top.dtype
    )
    factor = jnp.exp(request_top - global_top)
    cache_mixed, cache_sums = (
        lax.psum_scatter(
            factor[:, :, None] * request_mixed.reshape(requests, heads_total, HD),
            ("row", "col"),
            scatter_dimension=0,
            tiled=True,
        ),
        lax.psum_scatter(factor * request_sums, ("row", "col"), scatter_dimension=0, tiled=True),
    )
    cache_top = lax.dynamic_slice_in_dim(global_top, device_rank * req_local, req_local, 0)
    own_queries = queries.reshape(req_local, steps, KVH, groups, HD)
    fresh = new_kv.reshape(req_local, steps, 2, KVH, HD)
    fresh_scores = (
        jnp.einsum(
            "rskgd,rukd->rskgu", own_queries, fresh[:, :, 0], preferred_element_type=jnp.float32
        )
        * scale
    )
    causal = jnp.arange(steps)[None, :] <= jnp.arange(steps)[:, None]
    fresh_scores = jnp.where(causal[None, :, None, None, :], fresh_scores, floor_score).reshape(
        req_local, heads_total, steps
    )
    overall = jnp.maximum(cache_top, jnp.max(fresh_scores, axis=2))
    fresh_weights = jnp.exp(fresh_scores - overall[:, :, None])
    carried = jnp.exp(cache_top - overall)
    fresh_values = fresh[:, :, 1].astype(jnp.float32)
    fresh_mixed = jnp.einsum(
        "rskgu,rukd->rskgd",
        fresh_weights.reshape(req_local, steps, KVH, groups, steps),
        fresh_values,
        precision=lax.Precision.HIGHEST,
    )
    numerator = carried[:, :, None] * cache_mixed + fresh_mixed.reshape(req_local, heads_total, HD)
    denominator = carried * cache_sums + jnp.sum(fresh_weights, axis=2)
    tokens_here = req_local * steps
    attended = (
        (numerator / denominator[:, :, None]).reshape(tokens_here, width).astype(jnp.bfloat16)
    )
    column_slices = lax.all_to_all(attended, "col", split_axis=1, concat_axis=0, tiled=True)
    projected = lax.psum_scatter(
        jnp.dot(column_slices, w_out, preferred_element_type=jnp.float32).astype(jnp.bfloat16),
        "col",
        scatter_dimension=0,
        tiled=True,
    ).astype(jnp.float32)
    residual = (hidden_in.reshape(tokens_here, width).astype(jnp.float32) + projected).astype(
        jnp.bfloat16
    )
    stream = residual.astype(jnp.float32)
    normed = (
        stream
        * lax.rsqrt(jnp.mean(stream * stream, axis=1, keepdims=True) + 1e-05)
        * norm_gain.astype(jnp.float32)
    ).astype(jnp.bfloat16)
    picks = expert_ids.reshape(tokens_here * TOPK)
    onehot = (picks[:, None] == jnp.arange(EXPERTS, dtype=jnp.int32)[None, :]).astype(jnp.int32)
    earlier = jnp.cumsum(onehot, axis=0) - onehot
    slot_of = jnp.sum(earlier * onehot, axis=1)
    placed = onehot[:, :, None] * (
        slot_of[:, None, None] == jnp.arange(CAP, dtype=jnp.int32)[None, None, :]
    ).astype(jnp.int32)
    placed = placed.reshape(tokens_here, TOPK, EXPERTS, CAP)
    assign = jnp.sum(placed, axis=1).astype(jnp.bfloat16)
    outgoing = jnp.einsum("tec,td->ecd", assign, normed, preferred_element_type=jnp.float32).astype(
        jnp.bfloat16
    )
    row_count = lax.axis_size("row")
    local_experts = w_gate.shape[0]
    arriving = lax.all_to_all(outgoing, "row", split_axis=0, concat_axis=0, tiled=True)
    gathered = lax.all_gather(arriving, "col", axis=0, tiled=True)
    number = row_count * lax.axis_size("col")
    inputs = gathered.reshape(number, local_experts, CAP, width)
    inputs = jnp.transpose(inputs, (1, 0, 2, 3)).reshape(local_experts, number * CAP, width)
    gated = jnp.einsum("etd,edf->etf", inputs, w_gate, preferred_element_type=jnp.float32)
    upward = jnp.einsum("etd,edf->etf", inputs, w_up, preferred_element_type=jnp.float32)
    active = (jax.nn.silu(gated) * upward).astype(jnp.bfloat16)
    result = jnp.einsum("etf,efd->etd", active, w_down, preferred_element_type=jnp.float32)
    result = jnp.transpose(result.reshape(local_experts, number, CAP, width), (1, 0, 2, 3))
    expert_out = lax.psum_scatter(
        result.reshape(number, local_experts * CAP, width).astype(jnp.bfloat16),
        "col",
        scatter_dimension=0,
        tiled=True,
    )
    returned = lax.all_to_all(expert_out, "row", split_axis=0, concat_axis=0, tiled=True)
    weighting = jnp.sum(
        placed.astype(jnp.float32) * expert_gates.reshape(tokens_here, TOPK)[:, :, None, None],
        axis=1,
    )
    mixture = jnp.einsum(
        "tec,ecd->td", weighting, returned.astype(jnp.float32), precision=lax.Precision.HIGHEST
    )
    return (stream + mixture).astype(jnp.bfloat16).reshape(req_local, steps, width)


def solution(mesh):
    return jax.shard_map(
        on_device,
        mesh=mesh,
        in_specs=(
            P(("row", "col"), None, None),
            P(("row", "col"), None, None),
            P(("row", "col"), None, None),
            P(("row", "col"), None, None),
            P(),
            P(),
            P("col", None),
            P(),
            P(("row", "col"), None, None),
            P(("row", "col"), None, None),
            P("row", None, "col"),
            P("row", None, "col"),
            P("row", "col", None),
        ),
        out_specs=P(("row", "col"), None, None),
        check_vma=False,
    )
```

profile of v0, /device:TPU:0, one launch (start us, length us, event | category | flops | bytes accessed | tf_op | source)
XLA Modules:
  0.0 873.0 jit_solution(12035526291387564569)
XLA Ops:
  6.5 1.5 reshape.215
  8.1 1.7 fusion.52
  9.8 0.3 copy.230
  10.1 0.3 copy.231
  10.4 0.2 copy-done.1
  10.6 0.3 compare_reduce_fusion
  11.0 0.1 select_reduce_fusion.2
  11.1 0.8 fusion.7
  12.0 1.1 bitcast_bitcast_fusion.1
  13.0 1.1 bitcast_bitcast_fusion
  14.1 67.0 %all-gather.6.cloned.1.call-done = bf16[128,2,12288]{2,1,0:T(2,128)(2,1)} async-done(((bf16[1,2,12288]{2,1,0:T(2,128)(2,1)}), bf16[128,2,12288]{2,1,0:T(2,128)(2,1)}) %all-gather.6.cloned.1.call-update) | async-done | bytes 6291472 | tf_op jit(solution)/shard_map/all_gather | solution.py:58
  81.1 13.3 %reshape.216 = bf16[256,12288]{1,0:T(8,128)(2,1)} reshape(bf16[128,2,12288]{2,1,0:T(2,128)(2,1)} %all-gather.6.cloned.1.call-done) | data formatting | bytes 12582912
  94.4 3.9 convolution_convert_fusion
  98.3 1.2 reshape.201
  99.6 2.3 bitcast_reduce_fusion
  101.9 0.2 copy.179
  102.1 0.5 select_reduce_fusion.1
  102.7 0.6 select_reduce_fusion
  103.4 0.3 copy.187
  103.7 1.5 fusion.9
  105.2 0.2 copy.197
  105.4 63.4 %pmax.7 = bf16[256,96]{0,1:T(8,128)(2,1)S(1)} all-reduce(bf16[256,96]{0,1:T(8,128)(2,1)S(1)} %convert_element_type.84), channel_id=1, replica_groups=mesh['row'=8,'col'=16] {'row','col'}, use_global_device_ids=true, to_apply=%region_5.6 | all-reduce | flops 24576 | bytes 98304 | tf_op jit(solution)/shard_map/pmax | solution.py:85
  168.8 0.2 convolution_multiply_fusion
  169.0 0.7 copy.199
  169.8 0.2 reduce-scatter.3.cloned.1.call-start
  170.0 3.4 convolution_bitcast_fusion.1
  173.4 0.3 copy.189
  173.7 1.6 reshape.206
  175.3 8.7 broadcast_multiply_fusion
  184.0 16.5 %copy.191 = f32[256,96,128]{2,1,0:T(8,128)} copy(f32[256,96,128]{2,0,1:T(8,128)} %broadcast_multiply_fusion) | data formatting | bytes 25165824 | tf_op jit(solution)/shard_map/mul | solution.py:91
  200.5 0.8 copy-done.2
  201.4 0.4 fusion.54
  201.9 0.1 copy.184
  202.6 0.3 convolution_bitcast_fusion.2
  203.0 104.5 %all-reduce.7.cloned.1.call-done = f32[256,96]{1,0:T(8,128)} async-done(((f32[256,96]{1,0:T(8,128)}), f32[256,96]{1,0:T(8,128)}) %all-reduce.7.cloned.1.call-update) | async-done | bytes 98320
  307.5 0.7 constant_dynamic-slice_fusion.1
  308.5 223.8 %reduce-scatter.3.cloned.1.call-done = f32[2,96,128]{2,1,0:T(8,128)} async-done(((f32[256,96,128]{2,1,0:T(8,128)}), f32[2,96,128]{2,1,0:T(8,128)}) %reduce-scatter.3.cloned.1.call-update) | async-done | bytes 98320 | tf_op jit(solution)/shard_map/reduce_scatter | solution.py:90
  532.4 1.0 fusion.35
  533.4 0.6 copy.204
  534.1 4.8 all-to-all-start
  539.0 7.5 all-to-all-done
  546.5 4.2 convolution_convert_fusion.2
  550.9 0.6 dynamic-slice.1
  551.5 0.2 select_reduce_fusion.3
  552.8 80.4 %all-reduce.9.cloned.1.call-done = bf16[64,6144]{1,0:T(8,128)(2,1)} async-done(((bf16[64,6144]{1,0:T(8,128)(2,1)}), bf16[64,6144]{1,0:T(8,128)(2,1)}) %all-reduce.9.cloned.1.call-update) | async-done | bytes 786448
  633.3 1.1 fusion.31
  634.3 0.3 convolution_convert_fusion.3
  634.7 0.3 copy.208
  634.9 13.1 %all_to_all.26 = bf16[8,3,6144]{2,1,0:T(4,128)(2,1)S(1)} all-to-all(bf16[8,3,6144]{2,1,0:T(4,128)(2,1)S(1)} %copy.208), channel_id=1, replica_groups=mesh['row'=8,'col'=16] {'row'}, dimensions={0} | all-to-all | bytes 589824 | tf_op jit(solution)/shard_map/all_to_all | solution.py:157
  648.0 0.9 copy.209
  649.0 51.5 %all-gather.4.cloned.1.call-done = bf16[128,3,6144]{2,0,1:T(8,128)(2,1)} async-done(((bf16[8,3,6144]{2,0,1:T(8,128)(2,1)}), bf16[128,3,6144]{2,0,1:T(8,128)(2,1)}) %all-gather.4.cloned.1.call-update) | async-done | bytes 4718608 | tf_op jit(solution)/shard_map/all_gather | solution.py:158
  700.5 9.0 %copy.210 = bf16[128,3,6144]{2,1,0:T(4,128)(2,1)} copy(bf16[128,3,6144]{2,0,1:T(8,128)(2,1)} %all-gather.4.cloned.1.call-done) | data formatting | bytes 9437184 | tf_op jit(solution)/shard_map/all_gather | solution.py:158
  709.5 12.4 %reshape.209 = bf16[384,6144]{1,0:T(8,128)(2,1)} reshape(bf16[128,3,6144]{2,1,0:T(4,128)(2,1)} %copy.210) | data formatting | bytes 9437184 | tf_op jit(solution)/shard_map/reshape.2
  721.9 6.9 fusion.5
  728.9 5.5 fusion.16
  734.4 0.2 dot_general.58
  734.6 7.1 convolution_convert_fusion.1
  742.4 107.4 %all-reduce.11.cloned.1.call-done = bf16[128,3,6144]{2,0,1:T(8,128)(2,1)} async-done(((bf16[128,3,6144]{2,0,1:T(8,128)(2,1)}), bf16[128,3,6144]{2,0,1:T(8,128)(2,1)}) %all-reduce.11.cloned.1.call-update) | async-done | bytes 4718608
  849.8 1.0 constant_dynamic-slice_fusion
  850.8 1.0 copy.212
  851.8 4.3 all-to-all-start.2
  856.2 8.8 %all-to-all-done.2 = bf16[8,3,6144]{2,1,0:T(4,128)(2,1)S(1)} async-done(((bf16[8,3,6144]{2,1,0:T(4,128)(2,1)}), bf16[8,3,6144]{2,1,0:T(4,128)(2,1)S(1)}, u32[]{:S(2)}, u32[]{:S(2)}) %all-to-all-start.2) | async-done | bytes 294944 | tf_op jit(solution)/shard_map/all_to_all | solution.py:173
  865.0 0.5 fusion.1
  865.5 0.7 reshape.213
  (75 shorter events, 2.6 us)
Async XLA Ops:
  6.5 74.6 %all-gather.6.cloned.1.call-start = ((), (), s32[]{:S(2)}) async-start(), calls=%async_computation.6 | async-start | bytes 6340608 | tf_op jit(solution)/shard_map/all_gather | solution.py:58
  8.0 299.5 %all-reduce.7.cloned.1.call-start = ((), (), s32[]{:S(2)}) async-start(), calls=%async_computation.7 | async-start | bytes 262144
  9.8 0.8 copy-start.1
  9.8 1.2 copy-start.8
  169.8 362.6 %reduce-scatter.3.cloned.1.call-start = ((), (), s32[]{:S(2)}) async-start(), calls=%async_computation.4 | async-start | bytes 12681216 | tf_op jit(solution)/shard_map/reduce_scatter | solution.py:90
  200.5 0.8 copy-start.2
  200.5 0.8 copy-start.4
  200.5 338.4 %copy-start.6 = (s32[2,2,2]{2,1,0:T(2,128)S(1)}, s32[2,2,2]{2,1,0:T(2,128)}, u32[]{:S(2)}) copy-start(s32[2,2,2]{2,1,0:T(2,128)} %param.21) | copy-start | bytes 100
  534.1 12.4 %all-to-all-start = ((bf16[4,16,384]{2,0,1:T(4,128)(2,1)}), bf16[4,16,384]{2,0,1:T(4,128)(2,1)S(1)}, u32[]{:S(2)}, u32[]{:S(2)}) async-start(bf16[4,16,384]{2,0,1:T(4,128)(2,1)} %copy.204), calls=%async_computation.1 | async-start | bytes 98304 | tf_op jit(solution)/shard_map/all_to_all | solution.py:127
  538.8 94.4 %all-reduce.9.cloned.1.call-start = ((), (), s32[]{:S(2)}) async-start(), calls=%async_computation.8 | async-start | bytes 1572864
  546.5 4.4 copy-start.9
  546.5 5.0 copy-start.3
  546.5 5.5 copy-start.5
  550.8 149.7 %all-gather.4.cloned.1.call-start = ((), (), s32[]{:S(2)}) async-start(), calls=%async_computation.5 | async-start | bytes 5013504 | tf_op jit(solution)/shard_map/all_gather | solution.py:158
  648.9 200.8 %all-reduce.11.cloned.1.call-start = ((), (), s32[]{:S(2)}) async-start(), calls=%async_computation.9 | async-start | bytes 9437184
  721.9 6.9 copy-start
  741.7 114.3 %copy-start.7 = (f32[2,2,2]{2,1,0:T(2,128)S(1)}, f32[2,2,2]{2,1,0:T(2,128)}, u32[]{:S(2)}) copy-start(f32[2,2,2]{2,1,0:T(2,128)} %param.22) | copy-start | bytes 100
  851.8 13.2 %all-to-all-start.2 = ((bf16[8,3,6144]{2,1,0:T(4,128)(2,1)}), bf16[8,3,6144]{2,1,0:T(4,128)(2,1)S(1)}, u32[]{:S(2)}, u32[]{:S(2)}) async-start(bf16[8,3,6144]{2,1,0:T(4,128)(2,1)} %copy.212), calls=%async_computation.3 | async-start | bytes 786432 | tf_op jit(solution)/shard_map/all_to_all | solution.py:173
Sparse Core Ops, SparseCore 0:
  10.4 70.6 all-gather.5
  169.9 137.5 all-reduce.6
  313.3 219.0 reduce-scatter.2
  550.9 82.3 all-reduce.8
  649.1 51.3 all-gather.3
  741.9 107.8 all-reduce.10
where the time goes:
time: 875 us; the launch traced here: 873 us
  waiting for transfers between devices  651 us (74%)
  blocking collectives  76.5 us (9%)
  local copies, waits for them, and re-layouts  70.3 us (8%)
  matrix products  43.7 us (5%)
  between operations  15.2 us (2%)
  starting transfers between devices  9.44 us (1%)
    unnamed x9, waiting for transfers between devices  292 us
    reduce_scatter x1, waiting for transfers between devices, on_device(): lax.psum_scatter(factor[:, :, None] * request_mixed.reshape(requests, hea...  224 us
    all_gather x1, waiting for transfers between devices, on_device(): lax.all_gather(flat_queries, ('row', 'col'), axis=0, tiled=True)  67 us
    pmax x1, blocking collectives, on_device(): lax.pmax(request_top.astype(jnp.bfloat16), ('row', 'col'))  63.4 us
    all_gather x1, waiting for transfers between devices, on_device(): gathered = lax.all_gather(arriving, 'col', axis=0, tiled=True)  51.5 us
    unnamed x27, local copies, waits for them, and re-layouts  18.6 us
  transfers between devices with their start and end apart: 8, of which 8 were waited for; matrix products, arithmetic and copies ran while one was open for 5% of the time, Pallas kernels for 0%

commit v1 on v0

v1 whole, which is shorter than its diff:
```python
import jax, functools
import jax.numpy as jnp
from jax import lax
from jax.experimental import pallas as pl
from jax.experimental.pallas import tpu as pltpu
from jax.sharding import PartitionSpec as P

MESH = pl.DeviceIdType.MESH
ORDERS = (("x", "y", "z"), ("y", "z", "x"), ("z", "x", "y"))
F32, BF16 = jnp.float32, jnp.bfloat16


def where_am_i():
    r, c = lax.axis_index("row"), lax.axis_index("col")
    return {"y": r // 2, "k": r % 2, "x": c // 4, "z": c % 4}


def device(me, **moved):
    at = dict(me)
    for name, step in moved.items():
        at[name] = (me[name] + step) % (2 if name == "k" else 4)
    return (at["y"] * 2 + at["k"], at["x"] * 4 + at["z"])


def pick(sel, name):
    return sel.get(name, slice(None))


def block_of(ref, k, sel, part):
    return ref.at[(pick(sel, "y"), k, pick(sel, "x"), pick(sel, "z")) + part]


def remote(src, dst, send, recv, where):
    return pltpu.make_async_remote_copy(
        src_ref=src, dst_ref=dst, send_sem=send, recv_sem=recv, device_id=where, device_id_type=MESH
    )


def greet(me, plane=False):
    bar = pltpu.get_barrier_semaphore()
    count = 0
    for name in ("x", "y", "z"):
        for d in (1, 2, 3):
            pl.semaphore_signal(bar, inc=1, device_id=device(me, **{name: d}), device_id_type=MESH)
            count += 1
    pl.semaphore_signal(bar, inc=1, device_id=device(me, k=1), device_id_type=MESH)
    count += 1
    if plane:
        for dx in (1, 2, 3):
            for dz in (1, 2, 3):
                pl.semaphore_signal(bar, inc=1, device_id=device(me, x=dx, z=dz), device_id_type=MESH)
                count += 1
    pl.semaphore_wait(bar, count)


def shift(me, **moved):
    return {n: (me[n] - s) % 4 for n, s in moved.items()}


def gather_blocks(buf, me, parts, send, recv, cs, cr):
    k = me["k"]
    started = []

    def go(p, sel, moved, i):
        there = block_of(buf, k, sel, parts[p])
        copy = remote(there, there, send.at[p, i], recv.at[p, i], device(me, **moved))
        copy.start()
        started.append(copy)

    def landed(p, sel, i):
        here = block_of(buf, k, sel, parts[p])
        remote(here, here, send.at[p, i], recv.at[p, i], device(me, k=1)).wait_recv()

    def across(p, sel, i):
        there = block_of(buf, k, sel, parts[p])
        copy = remote(there, there, cs.at[p, i], cr.at[p, i], device(me, k=1))
        copy.start()
        started.append(copy)

    for p, (a, b, c) in enumerate(ORDERS):
        for d in (2, 1, 3):
            go(p, {n: me[n] for n in "xyz"}, {a: d}, d - 1)
    for p, (a, b, c) in enumerate(ORDERS):
        for d in (1, 3, 2):
            landed(p, {a: (me[a] - d) % 4, b: me[b], c: me[c]}, d - 1)
        line = {b: me[b], c: me[c]}
        for d in (2, 1, 3):
            go(p, line, {b: d}, 3 + d - 1)
        for d in (2, 1, 3):
            go(p, line, {c: d}, 6 + d - 1)
        across(p, line, 0)
    for d in (1, 3, 2):
        for p, (a, b, c) in enumerate(ORDERS):
            line = {b: (me[b] - d) % 4, c: me[c]}
            landed(p, line, 3 + d - 1)
            for e in (2, 1, 3):
                go(p, line, {c: e}, 9 + (d - 1) * 3 + e - 1)
            across(p, line, d)
    for e in (1, 3, 2):
        for p, (a, b, c) in enumerate(ORDERS):
            landed(p, {b: me[b], c: (me[c] - e) % 4}, 6 + e - 1)
            for d in (1, 3, 2):
                landed(p, {b: (me[b] - d) % 4, c: (me[c] - e) % 4}, 9 + (d - 1) * 3 + e - 1)
            across(p, {c: (me[c] - e) % 4}, 3 + e)
    other = 1 - k
    for p, (a, b, c) in enumerate(ORDERS):
        for i, sel in enumerate(
            [{b: me[b], c: me[c]}]
            + [{b: (me[b] - d) % 4, c: me[c]} for d in (1, 2, 3)]
            + [{c: (me[c] - e) % 4} for e in (1, 2, 3)]
        ):
            here = block_of(buf, other, sel, parts[p])
            remote(here, here, cs.at[p, i], cr.at[p, i], device(me, k=1)).wait_recv()
    for copy in started:
        copy.wait_send()


def send_core(buf, me, parts, core, cs, cr, p):
    copy = remote(
        buf.at[(slice(None), 1 - me["k"], slice(None), slice(None)) + parts[p]],
        core.at[(slice(None), slice(None), slice(None)) + parts[p]],
        cs.at[p], cr.at[p], device(me, k=1),
    )
    copy.start()
    return copy


def scatter_blocks(buf, me, parts, core, r1, r2, r3, send, recv, started):
    k = me["k"]

    def go(p, sel, moved, dst, i):
        copy = remote(block_of(buf, k, sel, parts[p]), dst, send.at[p, i], recv.at[p, i], device(me, **moved))
        copy.start()
        started.append(copy)

    def landed(p, dst, i):
        remote(dst, dst, send.at[p, i], recv.at[p, i], device(me, k=1)).wait_recv()

    def add_core(p, c, at):
        rest = [n for n in ("y", "x", "z") if n != c]

        def body(i, _):
            idx = {c: at, rest[0]: i // 4, rest[1]: i % 4}
            mine = (idx["y"], k, idx["x"], idx["z"]) + parts[p]
            theirs = (idx["y"], idx["x"], idx["z"]) + parts[p]
            buf[mine] = (buf[mine].astype(F32) + core[theirs].astype(F32)).astype(BF16)
            return 0

        lax.fori_loop(0, 16, body, 0)

    for p, (a, b, c) in enumerate(ORDERS):
        started[p].wait_recv()
        for d in (2, 1, 3):
            add_core(p, c, (me[c] + d) % 4)
            go(p, {c: (me[c] + d) % 4}, {c: d}, r1.at[p, d - 1], d - 1)
    for p, (a, b, c) in enumerate(ORDERS):
        add_core(p, c, me[c])
    for p, (a, b, c) in enumerate(ORDERS):
        for d in (1, 2, 3):
            landed(p, r1.at[p, d - 1], d - 1)
        rest = [n for n in ("y", "x", "z") if n != c]

        def body(i, _):
            idx = {c: me[c], rest[0]: i // 4, rest[1]: i % 4}
            mine = (idx["y"], k, idx["x"], idx["z"]) + parts[p]
            total = buf[mine].astype(F32)
            for d in range(3):
                total += r1[p, d, i // 4, i % 4].astype(F32)
            buf[mine] = total.astype(BF16)
            return 0

        lax.fori_loop(0, 16, body, 0)
        for d in (2, 1, 3):
            go(p, {c: me[c], b: (me[b] + d) % 4}, {b: d}, r2.at[p, d - 1], 3 + d - 1)
    for p, (a, b, c) in enumerate(ORDERS):
        for d in (1, 2, 3):
            landed(p, r2.at[p, d - 1], 3 + d - 1)
        for i in range(4):
            idx = {c: me[c], b: me[b], a: i}
            mine = (idx["y"], k, idx["x"], idx["z"]) + parts[p]
            total = buf[mine].astype(F32)
            for d in range(3):
                total += r2[p, d, i].astype(F32)
            buf[mine] = total.astype(BF16)
        for d in (2, 1, 3):
            go(p, {c: me[c], b: me[b], a: (me[a] + d) % 4}, {a: d}, r3.at[p, d - 1], 6 + d - 1)
    sums = []
    for p, (a, b, c) in enumerate(ORDERS):
        for d in (1, 2, 3):
            landed(p, r3.at[p, d - 1], 6 + d - 1)
        total = buf[(me["y"], k, me["x"], me["z"]) + parts[p]].astype(F32)
        for d in range(3):
            total += r3[p, d].astype(F32)
        sums.append(total)
    for copy in started:
        copy.wait_send()
    return sums


def lane_parts(n):
    w = n // 3
    return [(slice(None), slice(w * p, w * p + w)) for p in range(3)]


def gather_call(block, cid):
    rows, lanes = block.shape

    def kernel(x_ref, o_ref, buf, send, recv, cs, cr, ls):
        me = where_am_i()
        greet(me)
        buf[me["y"], me["k"], me["x"], me["z"]] = x_ref[...]
        gather_blocks(buf, me, lane_parts(lanes), send, recv, cs, cr)
        cp = pltpu.make_async_copy(buf, o_ref, ls)
        cp.start()
        cp.wait()

    return pl.pallas_call(
        kernel,
        out_shape=jax.ShapeDtypeStruct((4, 2, 4, 4, rows, lanes), block.dtype),
        in_specs=[pl.BlockSpec(memory_space=pltpu.VMEM)],
        out_specs=pl.BlockSpec(memory_space=pl.ANY),
        scratch_shapes=[
            pltpu.VMEM((4, 2, 4, 4, rows, lanes), block.dtype),
            pltpu.SemaphoreType.DMA((3, 18)), pltpu.SemaphoreType.DMA((3, 18)),
            pltpu.SemaphoreType.DMA((3, 7)), pltpu.SemaphoreType.DMA((3, 7)),
            pltpu.SemaphoreType.DMA,
        ],
        compiler_params=pltpu.CompilerParams(collective_id=cid, has_side_effects=True, vmem_limit_bytes=40 * 2**20),
    )(block)


def scatter_call(blocks, cid):
    rows, lanes = blocks.shape[-2:]
    w = lanes // 3

    def kernel(x_ref, o_ref, buf, core, r1, r2, r3, send, recv, cs, cr, ls):
        me = where_am_i()
        cp = pltpu.make_async_copy(x_ref, buf, ls)
        cp.start()
        greet(me)
        cp.wait()
        started = [send_core(buf, me, lane_parts(lanes), core, cs, cr, p) for p in range(3)]
        sums = scatter_blocks(buf, me, lane_parts(lanes), core, r1, r2, r3, send, recv, started)
        for p in range(3):
            o_ref[:, w * p : w * p + w] = sums[p]

    return pl.pallas_call(
        kernel,
        out_shape=jax.ShapeDtypeStruct((rows, lanes), F32),
        in_specs=[pl.BlockSpec(memory_space=pl.ANY)],
        out_specs=pl.BlockSpec(memory_space=pltpu.VMEM),
        scratch_shapes=[
            pltpu.VMEM((4, 2, 4, 4, rows, lanes), BF16),
            pltpu.VMEM((4, 4, 4, rows, lanes), BF16),
            pltpu.VMEM((3, 3, 4, 4, rows, w), BF16),
            pltpu.VMEM((3, 3, 4, rows, w), BF16),
            pltpu.VMEM((3, 3, rows, w), BF16),
            pltpu.SemaphoreType.DMA((3, 9)), pltpu.SemaphoreType.DMA((3, 9)),
            pltpu.SemaphoreType.DMA((3,)), pltpu.SemaphoreType.DMA((3,)),
            pltpu.SemaphoreType.DMA,
        ],
        compiler_params=pltpu.CompilerParams(collective_id=cid, has_side_effects=True, vmem_limit_bytes=40 * 2**20),
    )(blocks)


ANY = pl.BlockSpec(memory_space=pl.ANY)
VM = pl.BlockSpec(memory_space=pltpu.VMEM)
DMA = pltpu.SemaphoreType.DMA
XPARTS = [(slice(None), slice(0, 512)), (slice(None), slice(512, 1024)), (slice(None), slice(1024, 1664))]


def experts_kernel(xb, rb, wg_h, wu_h, wd_h, o_ref, X, WG, WU, WD, S, core, r1, r2, r3, accg, accu, act, scal, fout, fin,
                   wsem, gs, gr, gcs, gcr, ss_, sr, scs, scr, fs, fr):
    me = where_am_i()
    k = me["k"]
    loads = [pltpu.make_async_copy(h, v, wsem.at[i]) for i, (h, v) in enumerate(((wg_h, WG), (wu_h, WU), (wd_h, WD)))]
    for c in loads:
        c.start()
    greet(me)
    X[me["y"], k, me["x"], me["z"]] = xb[...]
    gather_blocks(X, me, XPARTS, gs, gr, gcs, gcr)
    loads[0].wait()
    loads[1].wait()
    parts = lane_parts(1536)
    expert = me["y"] * 2 + k
    started = []
    for half in range(2):
        kk = 1 - k if half == 0 else k
        extra = jnp.zeros((256, 128), F32)
        for z in range(4):
            extra += X[:, kk, :, z, :, 1536:1664].reshape(256, 128).astype(F32)
        lane = lax.broadcasted_iota(jnp.int32, (256, 128), 1)
        squares = jnp.sum(jnp.where(lane < 3, extra, 0.0), axis=1, keepdims=True)
        weight = jnp.sum(jnp.where((lane == 8 + expert) | (lane == 16 + expert), extra, 0.0), axis=1, keepdims=True)
        rs = lax.rsqrt(squares * (1.0 / 6144.0) + 1e-5)
        scal[0] = jnp.broadcast_to(rs, (256, 128))
        scal[1] = jnp.broadcast_to(weight, (256, 128))

        def body(z, _):
            rows = pl.ds(pl.multiple_of(z * 1536, 1536), 1536)
            x = X[:, kk, :, z, :, 0:1536].reshape(256, 1536)
            for n in range(2):
                cols = slice(256 * n, 256 * n + 256)
                g = jnp.dot(x, WG[rows, cols], preferred_element_type=F32)
                u = jnp.dot(x, WU[rows, cols], preferred_element_type=F32)
                keep = jnp.where(z == 0, 0.0, 1.0)
                accg[:, cols] = accg[:, cols] * keep + g
                accu[:, cols] = accu[:, cols] * keep + u
            return 0

        accg[...] = jnp.zeros_like(accg)
        accu[...] = jnp.zeros_like(accu)
        lax.fori_loop(0, 4, body, 0)
        rs = scal[0, :, 0:1]
        weight = scal[1, :, 0:1]
        g = accg[...] * rs
        act[...] = (g / (1.0 + jnp.exp(-g)) * (accu[...] * rs) * weight).astype(BF16)
        if half == 0:
            loads[2].wait()
        for p in range(3):
            def down(z, _):
                cols = pl.ds(pl.multiple_of(z * 1536 + 512 * p, 512), 512)
                r = jnp.dot(act[...], WD[:, cols], preferred_element_type=F32)
                S[:, kk, :, z, :, 512 * p : 512 * p + 512] = r.astype(BF16).reshape(4, 4, 16, 512)
                return 0

            lax.fori_loop(0, 4, down, 0)
            if half == 0:
                started.append(send_core(S, me, parts, core, scs, scr, p))
    sums = scatter_blocks(S, me, parts, core, r1, r2, r3, ss_, sr, started)
    total = jnp.concatenate(sums, axis=1) + rb[...].astype(F32)
    for z in range(4):
        rows = total[4 * z : 4 * z + 4]
        fout[z] = jnp.concatenate([rows[:, 384 * q : 384 * q + 384] for q in range(4)], axis=0).astype(BF16)
    outs = []
    for d in (2, 1, 3):
        c = remote(fout.at[(me["z"] + d) % 4], fin.at[me["z"]], fs.at[d - 1], fr.at[d - 1], device(me, z=d))
        c.start()
        outs.append(c)
    fin[me["z"]] = fout[me["z"]]
    for d in (1, 3, 2):
        there = fin.at[(me["z"] - d) % 4]
        remote(there, there, fs.at[d - 1], fr.at[d - 1], device(me, k=1)).wait_recv()
    for c in outs:
        c.wait_send()
    o_ref[...] = fin[...]


def experts_call(xb, rb, wg, wu, wd, cid):
    V = pltpu.VMEM
    return pl.pallas_call(
        experts_kernel,
        out_shape=jax.ShapeDtypeStruct((4, 16, 384), BF16),
        in_specs=[VM, VM, ANY, ANY, ANY],
        out_specs=VM,
        scratch_shapes=[
            V((4, 2, 4, 4, 16, 1664), BF16), V((6144, 512), BF16), V((6144, 512), BF16), V((512, 6144), BF16),
            V((4, 2, 4, 4, 16, 1536), BF16), V((4, 4, 4, 16, 1536), BF16),
            V((3, 3, 4, 4, 16, 512), BF16), V((3, 3, 4, 16, 512), BF16), V((3, 3, 16, 512), BF16),
            V((256, 512), F32), V((256, 512), F32), V((256, 512), BF16), V((2, 256, 128), F32),
            V((4, 16, 384), BF16), V((4, 16, 384), BF16),
            DMA((3,)), DMA((3, 18)), DMA((3, 18)), DMA((3, 7)), DMA((3, 7)), DMA((3, 9)), DMA((3, 9)), DMA((3,)), DMA((3,)),
            DMA((3,)), DMA((3,)),
        ],
        compiler_params=pltpu.CompilerParams(collective_id=cid, has_side_effects=True, vmem_limit_bytes=60 * 2**20),
    )(xb, rb, wg, wu, wd)


QPARTS = [(slice(64 * p, 64 * p + 64), slice(None)) for p in range(3)]
EMPTY = 34


def attend_kernel(req, seen, prev, last, qb, nk, nvt, hin, gain, gtile, kv_h, wo_h, xb_o, rb_o,
                  Q, A, KV, VT, WO, accs, ms, ls, Z, Zm, Zl, St, Cst, core, r1, r2, r3, s1, St2, s2, St3, s3, Wt,
                  U, G, H, O, Rv, hid, hrec,
                  lsem, gs, gr, gcs, gcr, ss_, sr, ts, tr, scs, scr, tcs, tcr, hs, hr, as_, ar, ps, pr):
    me = where_am_i()
    k = me["k"]
    kv_load = pltpu.make_async_copy(kv_h, KV, lsem.at[0])
    wo_load = pltpu.make_async_copy(wo_h, WO, lsem.at[1])
    kv_load.start()
    wo_load.start()
    greet(me, plane=True)
    started = []
    Q[me["y"], k, me["x"], me["z"]] = qb[...]
    gather_blocks(Q, me, QPARTS, gs, gr, gcs, gcr)
    for d in (1, 2, 3):
        c = remote(hin.at[(me["z"] + d) % 4], hrec.at[me["z"]], hs.at[d - 1], hr.at[d - 1], device(me, z=d))
        c.start()
        started.append(c)
    hrec[me["z"]] = hin[me["z"]]
    kv_load.wait()

    def turn(j, _):
        v = jnp.concatenate([KV[j, :, 1024 + 128 * g : 1152 + 128 * g] for g in range(8)], axis=0)
        VT[j] = v.astype(F32).T.astype(BF16)
        return 0

    lax.fori_loop(0, 32, turn, 0)

    lane = lax.broadcasted_iota(jnp.int32, (128, 192), 1)
    rowi = lax.broadcasted_iota(jnp.int32, (128, 192), 0)
    head_kv = ((lane // 64) * 16 + lane % 16) // 6
    lane_i = (lane // 32) % 2
    lane_s = (lane // 16) % 2
    same = jnp.where(head_kv == rowi // 16, rowi % 16, 99)

    def slot(j, _):
        rq = req[j]
        q = Q[rq // 64, (rq // 32) % 2, (rq // 8) % 4, (rq // 2) % 4]
        ks = jnp.concatenate([KV[j, :, 128 * g : 128 * g + 128] for g in range(8)], axis=0)
        st = lax.dot_general(ks, q, (((1,), (1,)), ((), ())), preferred_element_type=F32) * (128 ** -0.5)
        st = jnp.where((same < seen[j]) & (lane_i == rq % 2), st, -1e30)
        m = jnp.max(st, axis=0, keepdims=True)
        w = jnp.exp(st - m)
        accs[j] = jnp.dot(VT[j], w.astype(BF16), preferred_element_type=F32)
        ms[j] = m
        ls[j] = jnp.sum(w, axis=0, keepdims=True)
        return 0

    lax.fori_loop(0, 32, slot, 0)
    own = Q[me["y"], k, me["x"], me["z"]]
    for i in range(2):
        st = lax.dot_general(nk[i], own, (((1,), (1,)), ((), ())), preferred_element_type=F32) * (128 ** -0.5)
        r = rowi[:16]
        ok = (head_kv[:16] == r // 2) & (r % 2 <= lane_s[:16]) & (lane_i[:16] == i)
        st = jnp.where(ok, st, -1e30)
        m = jnp.max(st, axis=0, keepdims=True)
        w = jnp.exp(st - m)
        accs[32 + i] = jnp.dot(nvt[i], w.astype(BF16), preferred_element_type=F32)
        ms[32 + i] = m
        ls[32 + i] = jnp.sum(w, axis=0, keepdims=True)
        accs[EMPTY + i] = jnp.zeros((128, 192), F32)
        ms[EMPTY + i] = jnp.full((1, 192), -1e30, F32)
        ls[EMPTY + i] = jnp.zeros((1, 192), F32)

    def chain(j, _):
        pj = prev[j]
        i = req[j] % 2
        m0, m1 = ms[j], ms[pj]
        m = jnp.maximum(m0, m1)
        w0, w1 = jnp.exp(m0 - m), jnp.exp(m1 - m)
        acc = accs[j] * w0 + accs[pj] * w1
        l = ls[j] * w0 + ls[pj] * w1
        accs[j] = acc
        ms[j] = m
        ls[j] = l
        mine = lane_i == i
        acc = jnp.where(mine, acc, 0.0)
        m = jnp.where(mine[:1], m, 0.0)
        l = jnp.where(mine[:1], l, 0.0)
        for p in range(3):
            s = slice(64 * p, 64 * p + 64)
            Z[j, p] = jnp.concatenate([acc[:64, s], acc[64:, s]], axis=1).astype(BF16)
            Zm[j, p] = jnp.concatenate([m[:, s], m[:, s]], axis=1)
            Zl[j, p] = jnp.concatenate([l[:, s], l[:, s]], axis=1)
        return 0

    lax.fori_loop(0, 36, chain, 0)

    def spread(kk):
        def body(n, _):
            y, x, z = n // 16, (n // 4) % 4, n % 4
            rank = y * 32 + kk * 16 + x * 4 + z
            s0, s1_ = last[2 * rank], last[2 * rank + 1]
            at = {"y": y, "x": x, "z": z}
            for p, (a, b, c) in enumerate(ORDERS):
                A[y, kk, x, z, 64 * p : 64 * p + 64, :] = Z[s0, p] + Z[s1_, p]
                row = pl.ds(at[b] * 4 + at[a], 1)
                St[p, kk, at[c], 0, row, :] = Zm[s0, p] + Zm[s1_, p]
                St[p, kk, at[c], 1, row, :] = Zl[s0, p] + Zl[s1_, p]
            return 0

        lax.fori_loop(0, 64, body, 0)

    spread(1 - k)
    cores = []
    for p in range(3):
        c0 = send_core(A, me, QPARTS, core, scs, scr, p)
        c1 = remote(St.at[p, 1 - k], Cst.at[p], tcs.at[p], tcr.at[p], device(me, k=1))
        c1.start()
        cores.append((c0, c1))
        started.extend((c0, c1))
    spread(k)

    def go(p, sel, moved, dst, i, stat, sdst):
        c0 = remote(block_of(A, k, sel, QPARTS[p]), dst, ss_.at[p, i], sr.at[p, i], device(me, **moved))
        c1 = remote(stat, sdst, ts.at[p, i], tr.at[p, i], device(me, **moved))
        c0.start()
        c1.start()
        started.extend((c0, c1))

    def landed(p, dst, i, sdst):
        remote(dst, dst, ss_.at[p, i], sr.at[p, i], device(me, k=1)).wait_recv()
        remote(sdst, sdst, ts.at[p, i], tr.at[p, i], device(me, k=1)).wait_recv()

    def merge(stats):
        top = functools.reduce(jnp.maximum, [m for m, _ in stats])
        ws = [jnp.exp(m - top) for m, _ in stats]
        return top, sum(w * l for w, (_, l) in zip(ws, stats)), ws

    def others(c):
        return [n for n in ("y", "x", "z") if n != c]

    for p, (a, b, c) in enumerate(ORDERS):
        for copy in cores[p]:
            copy.wait_recv()
        for d in (2, 1, 3, 0):
            at = (me[c] + d) % 4
            top, tot, ws = merge([(St[p, k, at, 0], St[p, k, at, 1]), (Cst[p, at, 0], Cst[p, at, 1])])
            St[p, k, at, 0] = top
            St[p, k, at, 1] = tot
            for i, w in enumerate(ws):
                Wt[i] = w

            def body(n, _, at=at, p=p, a=a, b=b, c=c):
                idx = {c: at, b: n // 4, a: n % 4}
                row = pl.ds(n, 1)
                mine = (idx["y"], k, idx["x"], idx["z"]) + QPARTS[p]
                theirs = (idx["y"], idx["x"], idx["z"]) + QPARTS[p]
                A[mine] = (A[mine].astype(F32) * Wt[0, row, :] + core[theirs].astype(F32) * Wt[1, row, :]).astype(BF16)
                return 0

            lax.fori_loop(0, 16, body, 0)
            if d:
                go(p, {c: at}, {c: d}, r1.at[p, d - 1], d - 1, St.at[p, k, at], s1.at[p, d - 1])
    for p, (a, b, c) in enumerate(ORDERS):
        for d in (1, 2, 3):
            landed(p, r1.at[p, d - 1], d - 1, s1.at[p, d - 1])
        top, tot, ws = merge([(St[p, k, me[c], 0], St[p, k, me[c], 1])] + [(s1[p, d, 0], s1[p, d, 1]) for d in range(3)])
        for i, w in enumerate(ws):
            Wt[i] = w
        for i in range(4):
            St2[p, i, 0:4] = top[4 * i : 4 * i + 4]
            St2[p, i, 4:8] = tot[4 * i : 4 * i + 4]

        def body(n, _, p=p, a=a, b=b, c=c):
            idx = {c: me[c], b: n // 4, a: n % 4}
            rest = others(c)
            row = pl.ds(n, 1)
            mine = (idx["y"], k, idx["x"], idx["z"]) + QPARTS[p]
            t = A[mine].astype(F32) * Wt[0, row, :]
            for d in range(3):
                t += r1[p, d, idx[rest[0]], idx[rest[1]]].astype(F32) * Wt[d + 1, row, :]
            A[mine] = t.astype(BF16)
            return 0

        lax.fori_loop(0, 16, body, 0)
        for d in (2, 1, 3):
            at = (me[b] + d) % 4
            go(p, {c: me[c], b: at}, {b: d}, r2.at[p, d - 1], 2 + d, St2.at[p, at], s2.at[p, d - 1])
    for p, (a, b, c) in enumerate(ORDERS):
        for d in (1, 2, 3):
            landed(p, r2.at[p, d - 1], 2 + d, s2.at[p, d - 1])
        stats = [St2[p, me[b]]] + [s2[p, d] for d in range(3)]
        top, tot, ws = merge([(s[0:4], s[4:8]) for s in stats])
        for i in range(4):
            idx = {c: me[c], b: me[b], a: i}
            mine = (idx["y"], k, idx["x"], idx["z"]) + QPARTS[p]
            t = A[mine].astype(F32) * ws[0][i : i + 1]
            for d in range(3):
                t += r2[p, d, i].astype(F32) * ws[d + 1][i : i + 1]
            A[mine] = t.astype(BF16)
            St3[p, i, 0:1] = top[i : i + 1]
            St3[p, i, 1:2] = tot[i : i + 1]
        for d in (2, 1, 3):
            at = (me[a] + d) % 4
            go(p, {c: me[c], b: me[b], a: at}, {a: d}, r3.at[p, d - 1], 5 + d, St3.at[p, at], s3.at[p, d - 1])
    for p, (a, b, c) in enumerate(ORDERS):
        for d in (1, 2, 3):
            landed(p, r3.at[p, d - 1], 5 + d, s3.at[p, d - 1])
        stats = [St3[p, me[a]]] + [s3[p, d] for d in range(3)]
        top, tot, ws = merge([(s[0:1], s[1:2]) for s in stats])
        t = A[(me["y"], k, me["x"], me["z"]) + QPARTS[p]].astype(F32) * ws[0]
        for d in range(3):
            t += r3[p, d].astype(F32) * ws[d + 1]
        t = t / tot
        both = jnp.concatenate([t, pltpu.roll(t, 64, 1)], axis=0)
        U[64 * p : 64 * p + 64, :] = both.T[:64]
    for c in range(16):
        rows = []
        for hh in range(3):
            h = 3 * c + hh
            rows.append(U[pl.ds((h // 16) * 64 + h % 16, 4, stride=16), :])
        G[c] = jnp.concatenate(rows + [jnp.zeros((4, 128), F32)], axis=0).astype(BF16)
    col = me["x"] * 4 + me["z"]
    steps = [(dx, dz) for dz in (2, 1, 3, 0) for dx in (2, 1, 3, 0) if dx or dz]

    def peer(dx, dz):
        return ((me["x"] + dx) % 4) * 4 + (me["z"] + dz) % 4

    for dx, dz in steps:
        c = remote(G.at[peer(dx, dz)], H.at[col], as_.at[dx * 4 + dz], ar.at[dx * 4 + dz], device(me, x=dx, z=dz))
        c.start()
        started.append(c)
    H[col] = G[col]
    for d in (1, 2, 3):
        there = hrec.at[(me["z"] - d) % 4]
        remote(there, there, hs.at[d - 1], hr.at[d - 1], device(me, k=1)).wait_recv()
    for z in range(4):
        f = hrec[z].astype(F32)
        hid[4 * z : 4 * z + 4, :] = jnp.concatenate([f[4 * q : 4 * q + 4] for q in range(4)], axis=1)
    wo_load.wait()
    for dx, dz in steps:
        there = H.at[peer(-dx, -dz)]
        remote(there, there, as_.at[dx * 4 + dz], ar.at[dx * 4 + dz], device(me, k=1)).wait_recv()
    heads = []
    hf = [H[c].astype(F32) for c in range(16)]
    for hh in range(3):
        heads.append(jnp.concatenate([hf[c][4 * hh : 4 * hh + 4] for c in range(16)], axis=0).astype(BF16))
    lhs = jnp.concatenate(heads, axis=1)
    for dz in (2, 1, 3, 0):
        zz = (me["z"] + dz) % 4
        res = jnp.dot(lhs, WO[:, pl.ds(pl.multiple_of(zz * 1536, 1536), 1536)], preferred_element_type=F32).astype(BF16)
        for x in range(4):
            O[x, zz] = res[16 * x : 16 * x + 16]
        for dx in (2, 1, 3, 0):
            if dx or dz:
                c = remote(O.at[(me["x"] + dx) % 4, zz], Rv.at[col], ps.at[dx * 4 + dz], pr.at[dx * 4 + dz], device(me, x=dx, z=dz))
                c.start()
                started.append(c)
    Rv[col] = O[me["x"], me["z"]]
    for dx, dz in steps:
        there = Rv.at[peer(-dx, -dz)]
        remote(there, there, ps.at[dx * 4 + dz], pr.at[dx * 4 + dz], device(me, k=1)).wait_recv()
    total = Rv[0].astype(F32)
    for c in range(1, 16):
        total += Rv[c].astype(F32)
    res = (hid[...] + total).astype(BF16)
    rb_o[...] = res
    f = res.astype(F32)
    xb_o[:, 0:1536] = (f * gain[me["z"]]).astype(BF16)
    squares = jnp.sum(f * f, axis=1, keepdims=True)
    high = squares.astype(BF16).astype(F32)
    low = squares - high
    ln = lax.broadcasted_iota(jnp.int32, (16, 128), 1)
    tile = jnp.where(ln == 0, high, jnp.where(ln == 1, low, gtile[...].astype(F32)))
    xb_o[:, 1536:1664] = tile.astype(BF16)
    for c in started:
        c.wait_send()


def attend_call(req, seen, prev, last, qb, nk, nvt, hin, gain, gtile, kv, wo, cid):
    V = pltpu.VMEM
    SM = pl.BlockSpec(memory_space=pltpu.SMEM)
    return pl.pallas_call(
        attend_kernel,
        out_shape=(jax.ShapeDtypeStruct((16, 1664), BF16), jax.ShapeDtypeStruct((16, 1536), BF16)),
        in_specs=[SM] * 4 + [VM] * 6 + [ANY, ANY],
        out_specs=(VM, VM),
        scratch_shapes=[
            V((4, 2, 4, 4, 192, 128), BF16), V((4, 2, 4, 4, 192, 128), BF16), V((32, 16, 2048), BF16), V((32, 128, 128), BF16),
            V((384, 6144), BF16), V((36, 128, 192), F32), V((36, 1, 192), F32), V((36, 1, 192), F32),
            V((36, 3, 64, 128), BF16), V((36, 3, 1, 128), F32), V((36, 3, 1, 128), F32),
            V((3, 2, 4, 2, 16, 128), F32), V((3, 4, 2, 16, 128), F32), V((4, 4, 4, 192, 128), BF16),
            V((3, 3, 4, 4, 64, 128), BF16), V((3, 3, 4, 64, 128), BF16), V((3, 3, 64, 128), BF16),
            V((3, 3, 2, 16, 128), F32), V((3, 4, 8, 128), F32), V((3, 3, 8, 128), F32), V((3, 4, 8, 128), F32), V((3, 3, 8, 128), F32),
            V((4, 16, 128), F32), V((192, 128), F32), V((16, 16, 128), BF16), V((16, 16, 128), BF16),
            V((4, 4, 16, 1536), BF16), V((16, 16, 1536), BF16), V((16, 1536), F32), V((4, 16, 384), BF16),
            DMA((2,)), DMA((3, 18)), DMA((3, 18)), DMA((3, 7)), DMA((3, 7)), DMA((3, 9)), DMA((3, 9)), DMA((3, 9)), DMA((3, 9)),
            DMA((3,)), DMA((3,)), DMA((3,)), DMA((3,)), DMA((3,)), DMA((3,)), DMA((16,)), DMA((16,)), DMA((16,)), DMA((16,)),
        ],
        compiler_params=pltpu.CompilerParams(collective_id=cid, has_side_effects=True, vmem_limit_bytes=60 * 2**20),
    )(req, seen, prev, last, qb, nk, nvt, hin, gain, gtile, kv, wo)


def on_device(hidden_in, queries, new_kv, kv_pool, block_table, cached_len, w_out, norm_gain, expert_ids, expert_gates,
              w_gate, w_up, w_down):
    rank = lax.axis_index(("row", "col"))
    z = lax.axis_index("col") % 4
    requests, blocks = block_table.shape
    ids = jnp.arange(requests, dtype=jnp.int32)[:, None]
    places = jnp.arange(blocks, dtype=jnp.int32)[None, :]
    visible = jnp.clip(cached_len[:, None] - 16 * places, 0, 16)
    code = ids * 32 + visible
    slots = rank * 32 + jnp.arange(32, dtype=jnp.int32)
    found = jnp.max(jnp.where(block_table[None] == slots[:, None, None], code[None], -1), axis=(1, 2))
    own = rank * 2 + jnp.arange(2, dtype=jnp.int32)
    owner = jnp.concatenate([jnp.where(found >= 0, found // 32, -1), own])
    seen = jnp.concatenate([jnp.where(found >= 0, found % 32, 0), jnp.zeros((2,), jnp.int32)])
    js = jnp.arange(34, dtype=jnp.int32)
    earlier = (owner[:, None] == owner[None, :]) & (js[None, :] < js[:, None]) & (owner[:, None] >= 0)
    prev = jnp.max(jnp.where(earlier, js[None, :], -1), axis=1)
    prev = jnp.where(prev < 0, EMPTY, prev)
    rs = jnp.arange(256, dtype=jnp.int32)
    last = jnp.max(jnp.where(owner[None, :] == rs[:, None], js[None, :], -1), axis=1)
    last = jnp.where(last < 0, EMPTY + rs % 2, last)
    pair = jnp.arange(2, dtype=jnp.int32)
    req = jnp.concatenate([jnp.maximum(owner, 0), pair])
    prev = jnp.concatenate([prev, jnp.full((2,), EMPTY, jnp.int32)])
    qb = jnp.transpose(queries.reshape(2, 2, 3, 16, 128), (2, 0, 1, 3, 4)).reshape(192, 128)
    fresh = new_kv.reshape(2, 2, 2, 8, 128)
    nk = jnp.transpose(fresh[:, :, 0], (0, 2, 1, 3)).reshape(2, 16, 128)
    nvt = jnp.transpose(fresh[:, :, 1], (0, 3, 2, 1)).reshape(2, 128, 16)
    hin = jnp.transpose(hidden_in.reshape(4, 4, 4, 384), (1, 2, 0, 3)).reshape(4, 16, 384)
    gain = norm_gain.astype(F32).reshape(4, 1, 1536)
    picks, gates = expert_ids.reshape(4, 2), expert_gates.reshape(4, 2)
    dense = jnp.sum(jnp.where(picks[:, :, None] == jnp.arange(8)[None, None], gates[:, :, None], 0.0), axis=1)
    high = dense.astype(BF16).astype(F32)
    rows = jnp.concatenate([jnp.zeros((4, 8), F32), high, dense - high, jnp.zeros((4, 104), F32)], axis=1)
    gtile = jnp.where((jnp.arange(16) // 4 == z)[:, None], jnp.tile(rows, (4, 1)), 0.0).astype(BF16)
    xb, rb = attend_call(req, seen, prev, last, qb, nk, nvt, hin, gain, gtile, kv_pool, w_out, 0)
    o = experts_call(xb, rb, w_gate[0], w_up[0], w_down[0], 1)
    return jnp.transpose(o.reshape(4, 4, 4, 384), (2, 0, 1, 3)).reshape(2, 2, 6144)


def solution(mesh):
    both = ("row", "col")
    return jax.shard_map(
        on_device,
        mesh=mesh,
        in_specs=(P(both, None, None), P(both, None, None), P(both, None, None), P(both, None, None), P(), P(), P("col", None),
                  P(), P(both, None, None), P(both, None, None), P("row", None, "col"), P("row", None, "col"), P("row", "col", None)),
        out_specs=P(both, None, None),
        check_vma=False,
    )
```

time: 875 us -> 195 us (0.22)
  waiting for transfers between devices: 651 us -> 0 us
  Pallas kernels: 0 us -> 179 us
  blocking collectives: 76.5 us -> 0 us
  local copies, waits for them, and re-layouts: 70.3 us -> 9.25 us
  matrix products: 43.7 us -> 0 us
  between operations: 15.2 us -> 0.09 us
  starting transfers between devices: 9.44 us -> 0 us
    unnamed x9 -> x0, waiting for transfers between devices: 292 us -> none
    reduce_scatter x1 -> x0, waiting for transfers between devices: 224 us -> none  [on_device(): lax.psum_scatter(factor[:, :, None] * request_mixed.reshape(requests, hea...]
    pallas_call x0 -> x2, Pallas kernels: none -> 179 us  [the longest x1 104 us: attend_call(): pl.pallas_call(attend_kernel, out_shape=(jax.ShapeDtypeStruct((16, 1664),...]
    all_gather x2 -> x0, waiting for transfers between devices: 118 us -> none  [the longest x1 67 us: on_device(): lax.all_gather(flat_queries, ('row', 'col'), axis=0, tiled=True)]
    pmax x1 -> x0, blocking collectives: 63.4 us -> none  [on_device(): lax.pmax(request_top.astype(jnp.bfloat16), ('row', 'col'))]
    dot_general x13 -> x0, matrix products: 43.7 us -> none  [the longest x1 8.71 us: on_device(): jnp.dot(holder_single.T, slot_mixed.reshape(blocks_here, steps * width),...]
    unnamed x27 -> x2, local copies, waits for them, and re-layouts: 18.6 us -> 0.61 us
    mul x3 -> x0, local copies, waits for them, and re-layouts: 17.3 us -> none  [the longest x1 16.5 us: on_device(): factor[:, :, None] * request_mixed.reshape(requests, heads_total, HD)]
  transfers between devices with their start and end apart: 8 -> 0, of which waited for: 8 -> 0; matrix products, arithmetic and copies ran while one was open for 5% -> 0% of each run, Pallas kernels for 0% -> 0%
where the time goes in v1:
time: 195 us
  Pallas kernels  179 us (92%)
  local copies, waits for them, and re-layouts  9.25 us (5%)
  other arithmetic  6.19 us (3%)
    pallas_call x1, Pallas kernels, attend_call(): pl.pallas_call(attend_kernel, out_shape=(jax.ShapeDtypeStruct((16, 1664),...  104 us
    pallas_call x1, Pallas kernels, experts_call(): pl.pallas_call(experts_kernel, out_shape=jax.ShapeDtypeStruct((4, 16, 384...  75.3 us

profile of v1, /device:TPU:0, one launch (start us, length us, event | category | flops | bytes accessed | tf_op | source)
XLA Modules:
  0.0 194.6 jit_solution(6649239118189971882)
XLA Ops:
  0.0 0.1 pad.5.clone
  0.1 0.8 copy.43
  0.9 0.8 copy.44
  1.7 0.1 select_reduce_fusion.3
  1.8 0.1 maximum_maximum_fusion
  1.8 0.7 select_convert_fusion.gtile
  2.5 0.7 reshape.125
  3.3 0.6 copy.45
  3.9 1.3 reshape.134
  5.2 0.8 reshape.128
  6.1 0.6 reshape.129.hin
  6.7 0.8 reshape.123
  7.5 0.6 copy.35
  8.2 0.7 copy.41.nvt
  8.9 0.8 clamp_add_fusion
  9.6 1.6 select_reduce_fusion
  11.3 0.6 concatenate.21.seen
  11.9 0.1 broadcast_compare_fusion
  12.0 0.2 select_reduce_fusion.2
  12.2 0.5 concatenate.22.prev
  12.7 0.7 pad_add_fusion.1.req
  13.4 0.1 select_reduce_fusion.1
  13.4 0.6 compare_select_fusion.last
  14.0 103.8 %shard_map.127 = (bf16[16,1664]{1,0:T(8,128)(2,1)}, bf16[16,1536]{1,0:T(8,128)(2,1)}) custom-call(s32[36]{0:T(128)} %pad_add_fusion.1.req, s32[34]{0:T(128)} %concatenate.21.seen, s32[36]{0:T(128)} %concatenate.22.prev, s32[256]{0:T(256)} %compare_select_fusion.last, bf16[192,128]{1,0:T(8,128)(2,1)} %bitcast.27, bf16[2,16,128]{2,1,0:T(8,128)(2,1)} %bitcast.31, ...), custom_call_target="tpu_custom_call" | custom-call | tf_op jit(solution)/shard_map/pallas_call | solution.py:646
  117.8 75.3 %shard_map.128 = bf16[4,16,384]{2,1,0:T(8,128)(2,1)} custom-call(bf16[16,1664]{1,0:T(8,128)(2,1)} %get-tuple-element.7.xb, bf16[16,1536]{1,0:T(8,128)(2,1)} %get-tuple-element.8.rb, bf16[6144,512]{1,0:T(8,128)(2,1)} %bitcast.24, bf16[6144,512]{1,0:T(8,128)(2,1)} %bitcast.25, bf16[512,6144]{1,0:T(8,128)(2,1)} %bitcast.26), custom_call_target="tpu_custom_call" | custom-call | tf_op jit(solution)/shard_map/pallas_call | solution.py:351
  193.1 0.8 reshape.132
  193.9 0.6 reshape.133
  (19 shorter events, 0.1 us)

commit v2 on v1

v2 whole, which is shorter than its diff:
```python
import jax, functools
import jax.numpy as jnp
from jax import lax
from jax.experimental import pallas as pl
from jax.experimental.pallas import tpu as pltpu
from jax.sharding import PartitionSpec as P

MESH = pl.DeviceIdType.MESH
ORDERS = (("x", "y", "z"), ("y", "z", "x"), ("z", "x", "y"))
F32, BF16 = jnp.float32, jnp.bfloat16


def where_am_i():
    r, c = lax.axis_index("row"), lax.axis_index("col")
    return {"y": r // 2, "k": r % 2, "x": c // 4, "z": c % 4}


def device(me, **moved):
    at = dict(me)
    for name, step in moved.items():
        at[name] = (me[name] + step) % (2 if name == "k" else 4)
    return (at["y"] * 2 + at["k"], at["x"] * 4 + at["z"])


def pick(sel, name):
    return sel.get(name, slice(None))


def block_of(ref, k, sel, part):
    return ref.at[(pick(sel, "y"), k, pick(sel, "x"), pick(sel, "z")) + part]


def remote(src, dst, send, recv, where):
    return pltpu.make_async_remote_copy(
        src_ref=src, dst_ref=dst, send_sem=send, recv_sem=recv, device_id=where, device_id_type=MESH
    )


def greet(me, plane=False):
    bar = pltpu.get_barrier_semaphore()
    count = 0
    for name in ("x", "y", "z"):
        for d in (1, 2, 3):
            pl.semaphore_signal(bar, inc=1, device_id=device(me, **{name: d}), device_id_type=MESH)
            count += 1
    pl.semaphore_signal(bar, inc=1, device_id=device(me, k=1), device_id_type=MESH)
    count += 1
    if plane:
        for dx in (1, 2, 3):
            for dz in (1, 2, 3):
                pl.semaphore_signal(bar, inc=1, device_id=device(me, x=dx, z=dz), device_id_type=MESH)
                count += 1
    pl.semaphore_wait(bar, count)


def shift(me, **moved):
    return {n: (me[n] - s) % 4 for n, s in moved.items()}


HALF = (slice(0, 2), slice(2, 4))


def gather_blocks(buf, me, parts, send, recv, cs, cr, hooks=(), on_line=None):
    k = me["k"]
    started = []

    def go(p, sel, moved, i):
        there = block_of(buf, k, sel, parts[p])
        copy = remote(there, there, send.at[p, i], recv.at[p, i], device(me, **moved))
        copy.start()
        started.append(copy)

    def landed(p, sel, i):
        here = block_of(buf, k, sel, parts[p])
        remote(here, here, send.at[p, i], recv.at[p, i], device(me, k=1)).wait_recv()

    def across(p, sel, i, kk=k):
        there = block_of(buf, kk, sel, parts[p])
        return remote(there, there, cs.at[p, i], cr.at[p, i], device(me, k=1))

    def cross(p, sel, i):
        copy = across(p, sel, i)
        copy.start()
        started.append(copy)

    for p, (a, b, c) in enumerate(ORDERS):
        for d in (2, 1, 3):
            go(p, {n: me[n] for n in "xyz"}, {a: d}, d - 1)
    if hooks:
        hooks[0]()
    for p, (a, b, c) in enumerate(ORDERS):
        for d in (1, 3, 2):
            landed(p, {a: (me[a] - d) % 4, b: me[b], c: me[c]}, d - 1)
        for d in (2, 1, 3):
            go(p, {b: me[b], c: me[c]}, {b: d}, 3 + d - 1)
    if hooks:
        hooks[1]()
    for p, (a, b, c) in enumerate(ORDERS):
        for d in (1, 3, 2):
            landed(p, {b: (me[b] - d) % 4, c: me[c]}, 3 + d - 1)
        go(p, {b: HALF[0], c: me[c]}, {c: 1}, 6)
        go(p, {b: HALF[1], c: me[c]}, {c: -1}, 9)
        go(p, {b: HALF[1], c: me[c]}, {c: 1}, 7)
        go(p, {b: HALF[0], c: me[c]}, {c: -1}, 8)
        cross(p, {c: me[c]}, 0)
    if hooks:
        hooks[2]()

    def both_cores(i, d):
        for p, (a, b, c) in enumerate(ORDERS):
            across(p, {c: (me[c] + d) % 4}, i, 1 - k).wait_recv()
        if on_line:
            on_line(d)

    for p, (a, b, c) in enumerate(ORDERS):
        landed(p, {b: HALF[0], c: (me[c] - 1) % 4}, 6)
        go(p, {b: HALF[0], c: (me[c] - 1) % 4}, {c: 1}, 10)
        landed(p, {b: HALF[1], c: (me[c] + 1) % 4}, 9)
        go(p, {b: HALF[1], c: (me[c] + 1) % 4}, {c: -1}, 11)
    both_cores(0, 0)
    for p, (a, b, c) in enumerate(ORDERS):
        landed(p, {b: HALF[1], c: (me[c] - 1) % 4}, 7)
        cross(p, {c: (me[c] - 1) % 4}, 1)
        landed(p, {b: HALF[0], c: (me[c] + 1) % 4}, 8)
        cross(p, {c: (me[c] + 1) % 4}, 2)
    both_cores(1, 3)
    both_cores(2, 1)
    for p, (a, b, c) in enumerate(ORDERS):
        landed(p, {b: HALF[0], c: (me[c] + 2) % 4}, 10)
        landed(p, {b: HALF[1], c: (me[c] + 2) % 4}, 11)
        cross(p, {c: (me[c] + 2) % 4}, 3)
    both_cores(3, 2)
    for copy in started:
        copy.wait_send()


def send_core(buf, me, parts, core, cs, cr, p):
    copy = remote(
        buf.at[(slice(None), 1 - me["k"], slice(None), slice(None)) + parts[p]],
        core.at[(slice(None), slice(None), slice(None)) + parts[p]],
        cs.at[p], cr.at[p], device(me, k=1),
    )
    copy.start()
    return copy


def scatter_blocks(buf, me, parts, fwd, line, r2, r3, send, recv, started, ready):
    k = me["k"]

    def go(p, sel, moved, dst, i):
        copy = remote(block_of(buf, k, sel, parts[p]), dst, send.at[p, i], recv.at[p, i], device(me, **moved))
        copy.start()
        started.append(copy)

    def landed(p, dst, i):
        remote(dst, dst, send.at[p, i], recv.at[p, i], device(me, k=1)).wait_recv()

    def rest_of(c):
        return [n for n in ("y", "x", "z") if n != c]

    def sub(ref, p, j, b, c, half):
        return ref.at[(p, j) + tuple(HALF[half] if n == b else slice(None) for n in rest_of(c))]

    def add(p, b, c, at, half, terms):
        rest = rest_of(c)

        def body(n, _):
            i_b, i_a = 2 * half + n // 4, n % 4
            idx = {c: at, **{m: (i_b if m == b else i_a) for m in rest}}
            mine = (idx["y"], k, idx["x"], idx["z"]) + parts[p]
            total = buf[mine].astype(F32)
            for t in terms:
                total += t(idx, rest, n).astype(F32)
            buf[mine] = total.astype(BF16)
            return 0

        lax.fori_loop(0, 8, body, 0, unroll=4)

    for p, (a, b, c) in enumerate(ORDERS):
        ready(p)
        far, right, left = (me[c] + 2) % 4, (me[c] + 1) % 4, (me[c] - 1) % 4
        go(p, {c: far, b: HALF[0]}, {c: 1}, fwd_dst(fwd, p, 0, a, b, c), 0)
        go(p, {c: far, b: HALF[1]}, {c: -1}, fwd_dst(fwd, p, 1, a, b, c), 1)
        go(p, {c: right, b: HALF[1]}, {c: 1}, sub(line, p, 0, b, c, 1), 2)
        go(p, {c: left, b: HALF[0]}, {c: -1}, sub(line, p, 1, b, c, 0), 3)
    for p, (a, b, c) in enumerate(ORDERS):
        right, left = (me[c] + 1) % 4, (me[c] - 1) % 4
        landed(p, fwd_dst(fwd, p, 0, a, b, c), 0)
        add(p, b, c, right, 0, [fwd_at(fwd, p, 0, a, b, c)])
        go(p, {c: right, b: HALF[0]}, {c: 1}, sub(line, p, 0, b, c, 0), 4)
        landed(p, fwd_dst(fwd, p, 1, a, b, c), 1)
        add(p, b, c, left, 1, [fwd_at(fwd, p, 1, a, b, c)])
        go(p, {c: left, b: HALF[1]}, {c: -1}, sub(line, p, 1, b, c, 1), 5)
    for p, (a, b, c) in enumerate(ORDERS):
        for i, (j, h) in ((2, (0, 1)), (3, (1, 0)), (4, (0, 0)), (5, (1, 1))):
            landed(p, sub(line, p, j, b, c, h), i)
        def lt(j, p=p):
            return lambda idx, rest, n: line[p, j, idx[rest[0]], idx[rest[1]]]
        for h in range(2):
            add(p, b, c, me[c], h, [lt(0), lt(1)])
        for d in (2, 1, 3):
            go(p, {c: me[c], b: (me[b] + d) % 4}, {b: d}, r2.at[p, d - 1], 5 + d)
    for p, (a, b, c) in enumerate(ORDERS):
        for d in (1, 2, 3):
            landed(p, r2.at[p, d - 1], 5 + d)
        for i in range(4):
            idx = {c: me[c], b: me[b], a: i}
            mine = (idx["y"], k, idx["x"], idx["z"]) + parts[p]
            total = buf[mine].astype(F32)
            for d in range(3):
                total += r2[p, d, i].astype(F32)
            buf[mine] = total.astype(BF16)
        for d in (2, 1, 3):
            go(p, {c: me[c], b: me[b], a: (me[a] + d) % 4}, {a: d}, r3.at[p, d - 1], 8 + d)
    sums = []
    for p, (a, b, c) in enumerate(ORDERS):
        for d in (1, 2, 3):
            landed(p, r3.at[p, d - 1], 8 + d)
        total = buf[(me["y"], k, me["x"], me["z"]) + parts[p]].astype(F32)
        for d in range(3):
            total += r3[p, d].astype(F32)
        sums.append(total)
    for copy in started:
        copy.wait_send()
    return sums


def half_first(a, b, c):
    rest = [n for n in ("y", "x", "z") if n != c]
    return rest[0] == b


def fwd_dst(fwd, p, j, a, b, c):
    return fwd[half_first(a, b, c)].at[p, j]


def fwd_at(fwd, p, j, a, b, c):
    if half_first(a, b, c):
        return lambda idx, rest, n: fwd[True][p, j, n // 4, n % 4]
    return lambda idx, rest, n: fwd[False][p, j, n % 4, n // 4]


QPARTS = [(slice(64 * p, 64 * p + 64), slice(None)) for p in range(3)]
EMPTY = 34


def layer_kernel(table, clen, ids, gates, queries, new_kv, hidden, gain, kv_h, wo_h, wg_h, wu_h, wd_h, o_ref,
                 X, A, KV, VT, WO, WG, WU, WD, accs, ms, ls, Z, Zm, Zl, St, Cst, core, fa, fb, line, r2, r3, sf, sl, St2, s2, St3, s3, Wt,
                 U, NK, NV, GF, CC, info_v, info, G, H, O, Rv, hid, hin, hrec, acc, act, scal, resid, fout, fin,
                 lsem, gs, gr, gcs, gcr, ss_, sr, ts, tr, scs, scr, tcs, tcr, hs, hr, as_, ar, ps, pr,
                 gs2, gr2, gcs2, gcr2, ss2, sr2, scs2, scr2, fs, fr):
    me = where_am_i()
    k = me["k"]
    rank = me["y"] * 32 + k * 16 + me["x"] * 4 + me["z"]
    kv_load = pltpu.make_async_copy(kv_h, KV, lsem.at[0])
    wo_load = pltpu.make_async_copy(wo_h, WO, lsem.at[1])
    loads = [pltpu.make_async_copy(h.at[0], v, lsem.at[2 + i]) for i, (h, v) in enumerate(((wg_h, WG), (wu_h, WU), (wd_h, WD)))]
    info_load = pltpu.make_async_copy(info_v, info, lsem.at[5])
    kv_load.start()
    wo_load.start()
    for c in loads:
        c.start()
    for i in range(2):
        q = queries[i].astype(F32)
        for h in range(48):
            U[pl.ds((h // 16) * 64 + i * 32 + h % 16, 2, stride=16), :] = q[:, 128 * h : 128 * h + 128]
    X[me["y"], k, me["x"], me["z"], 0:192, :] = U[...].astype(BF16)
    greet(me, plane=True)
    started = []

    def find_blocks():
        code = lax.broadcasted_iota(jnp.int32, (64, 256), 1) * 64 + lax.broadcasted_iota(jnp.int32, (64, 256), 0)

        def search(j, _):
            CC[pl.ds(j, 1), :] = jnp.max(jnp.where(table[...] == rank * 32 + j, code, -1), axis=0, keepdims=True)
            return 0

        lax.fori_loop(0, 32, search, 0, unroll=4)
        CC[32:40, :] = jnp.full((8, 256), -1, jnp.int32)
        found = jnp.max(CC[...], axis=1, keepdims=True)
        r = lax.broadcasted_iota(jnp.int32, (40, 128), 0)
        c = lax.broadcasted_iota(jnp.int32, (40, 128), 1)
        found = jnp.broadcast_to(found, (40, 128))
        found = jnp.where((r == 32) | (r == 33), (rank * 2 + r - 32) * 64, found)
        owner = jnp.where(found >= 0, found // 64, -1)
        as_row = lambda v: jnp.max(jnp.where(r == c, v, -1), axis=0, keepdims=True)
        owner_row, place_row = as_row(owner), as_row(jnp.where(found >= 0, found % 64, 0))
        before = jnp.max(jnp.where((owner == owner_row) & (r < c) & (owner >= 0), r, -1), axis=0, keepdims=True)
        info_v[1:2, 0:128] = jnp.where(before < 0, EMPTY, before)
        cr = c[0:1]
        info_v[2:3, 0:128] = jnp.where(cr < 34, jnp.maximum(owner_row, 0), jnp.where(cr == 35, 1, 0))
        info_v[3:4, 0:128] = jnp.maximum(place_row, 0)
        r2_ = lax.broadcasted_iota(jnp.int32, (40, 256), 0)
        c2_ = lax.broadcasted_iota(jnp.int32, (40, 256), 1)
        owner2 = jnp.concatenate([owner, owner], axis=1)
        last_ = jnp.max(jnp.where(owner2 == c2_, r2_, -1), axis=0, keepdims=True)
        info_v[0:1, :] = jnp.where(last_ < 0, EMPTY + c2_[0:1] % 2, last_)
        info_load.start()

    def small_things():
        for i in range(2):
            v = new_kv[i].astype(F32)
            for g in range(8):
                NK[i, 2 * g : 2 * g + 2, :] = v[:, 128 * g : 128 * g + 128]
                NV[i, 2 * g : 2 * g + 2, :] = v[:, 1024 + 128 * g : 1152 + 128 * g]
        GF[...] = gain[...].astype(F32)
        f = jnp.concatenate([hidden[0].astype(F32), hidden[1].astype(F32)], axis=0)
        for z in range(4):
            hin[z] = jnp.concatenate([f[:, 1536 * z + 384 * q : 1536 * z + 384 * q + 384] for q in range(4)], axis=0).astype(BF16)
        for d in (1, 2, 3):
            c = remote(hin.at[(me["z"] + d) % 4], hrec.at[me["z"]], hs.at[d - 1], hr.at[d - 1], device(me, z=d))
            c.start()
            started.append(c)
        hrec[me["z"]] = hin[me["z"]]

    def turn_values():
        kv_load.wait()

        def turn(j, _):
            v = jnp.concatenate([KV[j, :, 1024 + 128 * g : 1152 + 128 * g] for g in range(8)], axis=0)
            VT[j] = v.astype(F32).T.astype(BF16)
            return 0

        lax.fori_loop(0, 32, turn, 0, unroll=4)
        fresh_slots()

    lane = lax.broadcasted_iota(jnp.int32, (128, 192), 1)
    rowi = lax.broadcasted_iota(jnp.int32, (128, 192), 0)
    head_kv = ((lane // 64) * 16 + lane % 16) // 6
    lane_i = (lane // 32) % 2
    lane_s = (lane // 16) % 2
    same = jnp.where(head_kv == rowi // 16, rowi % 16, 99)

    def fresh_slots():
        own = X[me["y"], k, me["x"], me["z"], 0:192, :]
        for i in range(2):
            st = lax.dot_general(NK[i].astype(BF16), own, (((1,), (1,)), ((), ())), preferred_element_type=F32) * (128 ** -0.5)
            r = rowi[:16]
            ok = (head_kv[:16] == r // 2) & (r % 2 <= lane_s[:16]) & (lane_i[:16] == i)
            st = jnp.where(ok, st, -1e30)
            m = jnp.max(st, axis=0, keepdims=True)
            w = jnp.exp(st - m)
            accs[32 + i] = jnp.dot(NV[i].T.astype(BF16), w.astype(BF16), preferred_element_type=F32)
            ms[32 + i] = m
            ls[32 + i] = jnp.sum(w, axis=0, keepdims=True)
            accs[EMPTY + i] = jnp.zeros((128, 192), F32)
            ms[EMPTY + i] = jnp.full((1, 192), -1e30, F32)
            ls[EMPTY + i] = jnp.zeros((1, 192), F32)

    gather_blocks(X, me, QPARTS, gs, gr, gcs, gcr, (find_blocks, small_things, turn_values))
    info_load.wait()

    def slot(j, _):
        rq = info[2, j]
        seen = jnp.clip(clen[rq] - 16 * info[3, j], 0, 16)
        q = X[rq // 64, (rq // 32) % 2, (rq // 8) % 4, (rq // 2) % 4, 0:192, :]
        ks = jnp.concatenate([KV[j, :, 128 * g : 128 * g + 128] for g in range(8)], axis=0)
        st = lax.dot_general(ks, q, (((1,), (1,)), ((), ())), preferred_element_type=F32) * (128 ** -0.5)
        st = jnp.where((same < seen) & (lane_i == rq % 2), st, -1e30)
        m = jnp.max(st, axis=0, keepdims=True)
        w = jnp.exp(st - m)
        accs[j] = jnp.dot(VT[j], w.astype(BF16), preferred_element_type=F32)
        ms[j] = m
        ls[j] = jnp.sum(w, axis=0, keepdims=True)
        return 0

    lax.fori_loop(0, 32, slot, 0, unroll=4)
    def chain(j, _):
        pj = info[1, j]
        i = info[2, j] % 2
        m0, m1 = ms[j], ms[pj]
        m = jnp.maximum(m0, m1)
        w0, w1 = jnp.exp(m0 - m), jnp.exp(m1 - m)
        acc = accs[j] * w0 + accs[pj] * w1
        l = ls[j] * w0 + ls[pj] * w1
        accs[j] = acc
        ms[j] = m
        ls[j] = l
        mine = lane_i == i
        acc = jnp.where(mine, acc, 0.0)
        m = jnp.where(mine[:1], m, 0.0)
        l = jnp.where(mine[:1], l, 0.0)
        for p in range(3):
            s = slice(64 * p, 64 * p + 64)
            Z[j, p] = jnp.concatenate([acc[:64, s], acc[64:, s]], axis=1).astype(BF16)
            Zm[j, p] = jnp.concatenate([m[:, s], m[:, s]], axis=1)
            Zl[j, p] = jnp.concatenate([l[:, s], l[:, s]], axis=1)
        return 0

    lax.fori_loop(0, 36, chain, 0, unroll=2)

    def spread(kk, ps_):
        def body(n, _):
            y, x, z = n // 16, (n // 4) % 4, n % 4
            to = y * 32 + kk * 16 + x * 4 + z
            s0, s1_ = info[0, 2 * to], info[0, 2 * to + 1]
            at = {"y": y, "x": x, "z": z}
            for p in ps_:
                a, b, c = ORDERS[p]
                A[y, kk, x, z, 64 * p : 64 * p + 64, :] = Z[s0, p] + Z[s1_, p]
                row = pl.ds((at[b] % 2) * 4 + at[a], 1)
                St[p, kk, at[c], at[b] // 2, 0, row, :] = Zm[s0, p] + Zm[s1_, p]
                St[p, kk, at[c], at[b] // 2, 1, row, :] = Zl[s0, p] + Zl[s1_, p]
            return 0

        lax.fori_loop(0, 64, body, 0, unroll=4)

    cores = []
    for p in range(3):
        spread(1 - k, (p,))
        c0 = send_core(A, me, QPARTS, core, scs, scr, p)
        c1 = remote(St.at[p, 1 - k], Cst.at[p], tcs.at[p], tcr.at[p], device(me, k=1))
        c1.start()
        cores.append((c0, c1))
        started.extend((c0, c1))
    spread(k, (0, 1, 2))

    def go(p, sel, moved, dst, i, stat, sdst):
        c0 = remote(block_of(A, k, sel, QPARTS[p]), dst, ss_.at[p, i], sr.at[p, i], device(me, **moved))
        c1 = remote(stat, sdst, ts.at[p, i], tr.at[p, i], device(me, **moved))
        c0.start()
        c1.start()
        started.extend((c0, c1))

    def landed(p, dst, i, sdst):
        remote(dst, dst, ss_.at[p, i], sr.at[p, i], device(me, k=1)).wait_recv()
        remote(sdst, sdst, ts.at[p, i], tr.at[p, i], device(me, k=1)).wait_recv()

    def merge(stats):
        top = functools.reduce(jnp.maximum, [m for m, _ in stats])
        ws = [jnp.exp(m - top) for m, _ in stats]
        return top, sum(w * l for w, (_, l) in zip(ws, stats)), ws

    def others(c):
        return [n for n in ("y", "x", "z") if n != c]

    fwd = {True: fa, False: fb}

    def half_line(p, j, b, c, h):
        return line.at[(p, j) + tuple(HALF[h] if n == b else slice(None) for n in others(c))]

    def blend(p, at, h, sources):
        a, b, c = ORDERS[p]
        here = St[p, k, at, h]
        stats = [(here[0], here[1])] + [(s[0], s[1]) for _, s in sources]
        top, tot, ws = merge(stats)
        St[p, k, at, h, 0] = top
        St[p, k, at, h, 1] = tot
        for i, w in enumerate(ws):
            Wt[i] = w

        def body(n, _):
            idx = {c: at, b: 2 * h + n // 4, a: n % 4}
            row = pl.ds(n, 1)
            mine = (idx["y"], k, idx["x"], idx["z"]) + QPARTS[p]
            t = A[mine].astype(F32) * Wt[0, row, :]
            for i, (block, _) in enumerate(sources):
                t += block(idx, n).astype(F32) * Wt[i + 1, row, :]
            A[mine] = t.astype(BF16)
            return 0

        lax.fori_loop(0, 8, body, 0, unroll=4)

    def from_core(p, at, h):
        return (lambda idx, n: core[(idx["y"], idx["x"], idx["z"]) + QPARTS[p]]), Cst[p, at, h]

    def from_fwd(p, j):
        a, b, c = ORDERS[p]
        get = fwd_at(fwd, p, j, a, b, c)
        return (lambda idx, n: get(idx, None, n)), sf[p, j]

    def from_line(p, j, h):
        rest = others(ORDERS[p][2])
        return (lambda idx, n: line[p, j, idx[rest[0]], idx[rest[1]]]), sl[p, j, h]

    for p, (a, b, c) in enumerate(ORDERS):
        for copy in cores[p]:
            copy.wait_recv()
        far, right, left = (me[c] + 2) % 4, (me[c] + 1) % 4, (me[c] - 1) % 4
        blend(p, far, 0, [from_core(p, far, 0)])
        go(p, {c: far, b: HALF[0]}, {c: 1}, fwd_dst(fwd, p, 0, a, b, c), 0, St.at[p, k, far, 0], sf.at[p, 0])
        blend(p, far, 1, [from_core(p, far, 1)])
        go(p, {c: far, b: HALF[1]}, {c: -1}, fwd_dst(fwd, p, 1, a, b, c), 1, St.at[p, k, far, 1], sf.at[p, 1])
        blend(p, right, 1, [from_core(p, right, 1)])
        go(p, {c: right, b: HALF[1]}, {c: 1}, half_line(p, 0, b, c, 1), 2, St.at[p, k, right, 1], sl.at[p, 0, 1])
        blend(p, left, 0, [from_core(p, left, 0)])
        go(p, {c: left, b: HALF[0]}, {c: -1}, half_line(p, 1, b, c, 0), 3, St.at[p, k, left, 0], sl.at[p, 1, 0])
    for p, (a, b, c) in enumerate(ORDERS):
        right, left = (me[c] + 1) % 4, (me[c] - 1) % 4
        landed(p, fwd_dst(fwd, p, 0, a, b, c), 0, sf.at[p, 0])
        blend(p, right, 0, [from_core(p, right, 0), from_fwd(p, 0)])
        go(p, {c: right, b: HALF[0]}, {c: 1}, half_line(p, 0, b, c, 0), 4, St.at[p, k, right, 0], sl.at[p, 0, 0])
        landed(p, fwd_dst(fwd, p, 1, a, b, c), 1, sf.at[p, 1])
        blend(p, left, 1, [from_core(p, left, 1), from_fwd(p, 1)])
        go(p, {c: left, b: HALF[1]}, {c: -1}, half_line(p, 1, b, c, 1), 5, St.at[p, k, left, 1], sl.at[p, 1, 1])
    for p, (a, b, c) in enumerate(ORDERS):
        for h in range(2):
            blend(p, me[c], h, [from_core(p, me[c], h)])
    for p, (a, b, c) in enumerate(ORDERS):
        for i, (j, h) in ((2, (0, 1)), (3, (1, 0)), (4, (0, 0)), (5, (1, 1))):
            landed(p, half_line(p, j, b, c, h), i, sl.at[p, j, h])
        for h in range(2):
            blend(p, me[c], h, [from_line(p, 0, h), from_line(p, 1, h)])
            for i in range(2):
                St2[p, 2 * h + i, 0:4] = St[p, k, me[c], h, 0, 4 * i : 4 * i + 4]
                St2[p, 2 * h + i, 4:8] = St[p, k, me[c], h, 1, 4 * i : 4 * i + 4]
        for d in (2, 1, 3):
            at = (me[b] + d) % 4
            go(p, {c: me[c], b: at}, {b: d}, r2.at[p, d - 1], 5 + d, St2.at[p, at], s2.at[p, d - 1])
    for p, (a, b, c) in enumerate(ORDERS):
        for d in (1, 2, 3):
            landed(p, r2.at[p, d - 1], 5 + d, s2.at[p, d - 1])
        stats = [St2[p, me[b]]] + [s2[p, d] for d in range(3)]
        top, tot, ws = merge([(s[0:4], s[4:8]) for s in stats])
        for i in range(4):
            idx = {c: me[c], b: me[b], a: i}
            mine = (idx["y"], k, idx["x"], idx["z"]) + QPARTS[p]
            t = A[mine].astype(F32) * ws[0][i : i + 1]
            for d in range(3):
                t += r2[p, d, i].astype(F32) * ws[d + 1][i : i + 1]
            A[mine] = t.astype(BF16)
            St3[p, i, 0:1] = top[i : i + 1]
            St3[p, i, 1:2] = tot[i : i + 1]
        for d in (2, 1, 3):
            at = (me[a] + d) % 4
            go(p, {c: me[c], b: me[b], a: at}, {a: d}, r3.at[p, d - 1], 8 + d, St3.at[p, at], s3.at[p, d - 1])
    for p, (a, b, c) in enumerate(ORDERS):
        for d in (1, 2, 3):
            landed(p, r3.at[p, d - 1], 8 + d, s3.at[p, d - 1])
        stats = [St3[p, me[a]]] + [s3[p, d] for d in range(3)]
        top, tot, ws = merge([(s[0:1], s[1:2]) for s in stats])
        t = A[(me["y"], k, me["x"], me["z"]) + QPARTS[p]].astype(F32) * ws[0]
        for d in range(3):
            t += r3[p, d].astype(F32) * ws[d + 1]
        t = t / tot
        both = jnp.concatenate([t, pltpu.roll(t, 64, 1)], axis=0)
        U[64 * p : 64 * p + 64, :] = both.T[:64]
    for c in range(16):
        rows = []
        for hh in range(3):
            h = 3 * c + hh
            rows.append(U[pl.ds((h // 16) * 64 + h % 16, 4, stride=16), :])
        G[c] = jnp.concatenate(rows + [jnp.zeros((4, 128), F32)], axis=0).astype(BF16)
    col = me["x"] * 4 + me["z"]
    steps = [(dx, dz) for dz in (2, 1, 3, 0) for dx in (2, 1, 3, 0) if dx or dz]

    def peer(dx, dz):
        return ((me["x"] + dx) % 4) * 4 + (me["z"] + dz) % 4

    for dx, dz in steps:
        c = remote(G.at[peer(dx, dz)], H.at[col], as_.at[dx * 4 + dz], ar.at[dx * 4 + dz], device(me, x=dx, z=dz))
        c.start()
        started.append(c)
    H[col] = G[col]
    for d in (1, 2, 3):
        there = hrec.at[(me["z"] - d) % 4]
        remote(there, there, hs.at[d - 1], hr.at[d - 1], device(me, k=1)).wait_recv()
    for z in range(4):
        f = hrec[z].astype(F32)
        hid[4 * z : 4 * z + 4, :] = jnp.concatenate([f[4 * q : 4 * q + 4] for q in range(4)], axis=1)
    wo_load.wait()
    for dx, dz in steps:
        there = H.at[peer(-dx, -dz)]
        remote(there, there, as_.at[dx * 4 + dz], ar.at[dx * 4 + dz], device(me, k=1)).wait_recv()
    heads = []
    hf = [H[c].astype(F32) for c in range(16)]
    for hh in range(3):
        heads.append(jnp.concatenate([hf[c][4 * hh : 4 * hh + 4] for c in range(16)], axis=0).astype(BF16))
    lhs = jnp.concatenate(heads, axis=1)
    for dz in (2, 1, 3, 0):
        zz = (me["z"] + dz) % 4
        res = jnp.dot(lhs, WO[:, pl.ds(pl.multiple_of(zz * 1536, 1536), 1536)], preferred_element_type=F32).astype(BF16)
        for x in range(4):
            O[x, zz] = res[16 * x : 16 * x + 16]
        for dx in (2, 1, 3, 0):
            if dx or dz:
                c = remote(O.at[(me["x"] + dx) % 4, zz], Rv.at[col], ps.at[dx * 4 + dz], pr.at[dx * 4 + dz], device(me, x=dx, z=dz))
                c.start()
                started.append(c)
    Rv[col] = O[me["x"], me["z"]]
    for dx, dz in steps:
        there = Rv.at[peer(-dx, -dz)]
        remote(there, there, ps.at[dx * 4 + dz], pr.at[dx * 4 + dz], device(me, k=1)).wait_recv()
    total = Rv[0].astype(F32)
    for c in range(1, 16):
        total += Rv[c].astype(F32)
    res = (hid[...] + total).astype(BF16)
    resid[...] = res
    f = res.astype(F32)
    xg = jnp.concatenate([f[:, 128 * c : 128 * c + 128] * GF[pl.ds(me["z"] * 12 + c, 1), :] for c in range(12)], axis=1).astype(BF16)
    squares = jnp.sum(f * f, axis=1, keepdims=True)
    high = squares.astype(BF16).astype(F32)
    low = squares - high
    ln = lax.broadcasted_iota(jnp.int32, (16, 128), 1)
    rw = lax.broadcasted_iota(jnp.int32, (16, 128), 0)
    gt = jnp.zeros((16, 128), F32)
    for t in range(4):
        for n in range(2):
            gt += jnp.where((rw == 4 * me["z"] + t) & (ln == 8 + ids[t // 2, t % 2, n]), gates[t // 2, t % 2, n], 0.0)
    gh = gt.astype(BF16).astype(F32)
    tile = gh + pltpu.roll(gt - gh, 8, 1)
    tile = jnp.where(ln == 0, high, jnp.where(ln == 1, low, tile)).astype(BF16)
    here = (me["y"], k, me["x"], me["z"])
    for c in range(12):
        X[here + (slice(16 * c, 16 * c + 16), slice(None))] = xg[:, 128 * c : 128 * c + 128]
    X[here + (slice(192, 208), slice(None))] = tile
    for c in started:
        c.wait_send()
    experts(me, X, WG, WU, WD, A, core, fwd, line, r2, r3, acc, act, scal, resid, fout, fin, loads,
            gs2, gr2, gcs2, gcr2, ss2, sr2, scs2, scr2, fs, fr, o_ref)


XPARTS = [(slice(0, 64), slice(None)), (slice(64, 128), slice(None)), (slice(128, 208), slice(None))]


def experts(me, X, WG, WU, WD, A, core, fwd, line, r2, r3, acc, act, scal, resid, fout, fin, loads,
            gs, gr, gcs, gcr, ss_, sr, scs, scr, fs, fr, o_ref):
    k = me["k"]
    expert = me["y"] * 2 + k
    acc[...] = jnp.zeros_like(acc)

    def add_product(at, rows, k0):
        x = jnp.concatenate([X[rows + (slice(16 * n, 16 * n + 16), slice(None))] for n in range(4 * k0[1], 4 * k0[1] + 4)], axis=-1)
        lead = x.shape[:-1]
        x = x.reshape(-1, 512)
        depth = pl.ds(pl.multiple_of(k0[0] * 1536 + 512 * k0[1], 512), 512)
        for n, W in enumerate((WG, WU)):
            for h in range(2):
                cols = slice(512 * n + 256 * h, 512 * n + 256 * h + 256)
                r = jnp.dot(x, W[depth, 256 * h : 256 * h + 256], preferred_element_type=F32)
                acc[at + (cols,)] += r.reshape(lead + (256,))

    def on_line(d):
        if d == 0:
            loads[0].wait()
            loads[1].wait()
        full = slice(None)
        z, x, y = (me["z"] + d) % 4, (me["x"] + d) % 4, (me["y"] + d) % 4
        add_product((full, full, full, full), (full, full, full, z), (z, 0))

        def body(zz, _):
            add_product((full, full, x, full), (full, full, x, zz), (zz, 1))
            add_product((y, full, full, full), (y, full, full, zz), (zz, 2))
            return 0

        lax.fori_loop(0, 4, body, 0)

    gather_blocks(X, me, XPARTS, gs, gr, gcs, gcr, (), on_line)
    loads[2].wait()
    extra = jnp.zeros((512, 128), F32)
    for z in range(4):
        extra += X[:, :, :, z, 192:208, :].reshape(512, 128).astype(F32)
    lane = lax.broadcasted_iota(jnp.int32, (512, 128), 1)
    squares = jnp.sum(jnp.where(lane < 3, extra, 0.0), axis=1, keepdims=True)
    weight = jnp.sum(jnp.where((lane == 8 + expert) | (lane == 16 + expert), extra, 0.0), axis=1, keepdims=True)
    scal[0] = jnp.broadcast_to(lax.rsqrt(squares * (1.0 / 6144.0) + 1e-5), (512, 128)).reshape(4, 2, 4, 16, 128)
    scal[1] = jnp.broadcast_to(weight, (512, 128)).reshape(4, 2, 4, 16, 128)
    started = []
    for kk in (1 - k, k):
        for n in range(4):
            at = (slice(None), kk, slice(None), slice(None))
            rs = scal[(0,) + at].reshape(256, 128)
            g = acc[at + (slice(128 * n, 128 * n + 128),)].reshape(256, 128) * rs
            u = acc[at + (slice(512 + 128 * n, 640 + 128 * n),)].reshape(256, 128) * rs
            v = g / (1.0 + jnp.exp(-g)) * u * scal[(1,) + at].reshape(256, 128)
            act[at + (slice(128 * n, 128 * n + 128),)] = v.astype(BF16).reshape(4, 4, 16, 128)

    def down(kk, p, with_core):
        def body(z, _):
            cols = pl.ds(pl.multiple_of(z * 1536 + 512 * p, 512), 512)
            r = jnp.dot(act[:, kk].reshape(256, 512), WD[:, cols], preferred_element_type=F32)
            for n in range(4):
                rows = slice(64 * p + 16 * n, 64 * p + 16 * n + 16)
                t = r[:, 128 * n : 128 * n + 128].reshape(4, 4, 16, 128)
                if with_core:
                    t += core[:, :, z, rows, :].astype(F32)
                A[:, kk, :, z, rows, :] = t.astype(BF16)
            return 0

        lax.fori_loop(0, 4, body, 0)

    for p in range(3):
        down(1 - k, p, False)
        started.append(send_core(A, me, QPARTS, core, scs, scr, p))

    def ready(p):
        started[p].wait_recv()
        down(k, p, True)

    sums = scatter_blocks(A, me, QPARTS, fwd, line, r2, r3, ss_, sr, started, ready)
    total = jnp.concatenate([s[16 * c : 16 * c + 16] for s in sums for c in range(4)], axis=1) + resid[...].astype(F32)
    for z in range(4):
        rows = total[4 * z : 4 * z + 4]
        fout[z] = jnp.concatenate([rows[:, 384 * q : 384 * q + 384] for q in range(4)], axis=0).astype(BF16)
    outs = []
    for d in (2, 1, 3):
        c = remote(fout.at[(me["z"] + d) % 4], fin.at[me["z"]], fs.at[d - 1], fr.at[d - 1], device(me, z=d))
        c.start()
        outs.append(c)
    fin[me["z"]] = fout[me["z"]]
    for d in (1, 3, 2):
        there = fin.at[(me["z"] - d) % 4]
        remote(there, there, fs.at[d - 1], fr.at[d - 1], device(me, k=1)).wait_recv()
    for c in outs:
        c.wait_send()
    for z in range(4):
        f = fin[z].astype(F32)
        rows = jnp.concatenate([f[4 * q : 4 * q + 4] for q in range(4)], axis=1).astype(BF16)
        o_ref[0, :, 1536 * z : 1536 * z + 1536] = rows[0:2]
        o_ref[1, :, 1536 * z : 1536 * z + 1536] = rows[2:4]


ANY = pl.BlockSpec(memory_space=pl.ANY)
VM = pl.BlockSpec(memory_space=pltpu.VMEM)
SM = pl.BlockSpec(memory_space=pltpu.SMEM)
DMA = pltpu.SemaphoreType.DMA


def on_device(hidden_in, queries, new_kv, kv_pool, block_table, cached_len, w_out, norm_gain, expert_ids, expert_gates,
              w_gate, w_up, w_down):
    V = pltpu.VMEM
    return pl.pallas_call(
        layer_kernel,
        out_shape=jax.ShapeDtypeStruct((2, 2, 6144), BF16),
        in_specs=[VM, SM, SM, SM, VM, VM, VM, VM] + [ANY] * 5,
        out_specs=VM,
        scratch_shapes=[
            V((4, 2, 4, 4, 208, 128), BF16), V((4, 2, 4, 4, 192, 128), BF16), V((32, 16, 2048), BF16), V((32, 128, 128), BF16),
            V((384, 6144), BF16), V((6144, 512), BF16), V((6144, 512), BF16), V((512, 6144), BF16),
            V((36, 128, 192), F32), V((36, 1, 192), F32), V((36, 1, 192), F32),
            V((36, 3, 64, 128), BF16), V((36, 3, 1, 128), F32), V((36, 3, 1, 128), F32),
            V((3, 2, 4, 2, 2, 8, 128), F32), V((3, 4, 2, 2, 8, 128), F32), V((4, 4, 4, 192, 128), BF16),
            V((3, 2, 2, 4, 64, 128), BF16), V((3, 2, 4, 2, 64, 128), BF16), V((3, 2, 4, 4, 64, 128), BF16),
            V((3, 3, 4, 64, 128), BF16), V((3, 3, 64, 128), BF16),
            V((3, 2, 2, 8, 128), F32), V((3, 2, 2, 2, 8, 128), F32), V((3, 4, 8, 128), F32), V((3, 3, 8, 128), F32), V((3, 4, 8, 128), F32), V((3, 3, 8, 128), F32),
            V((4, 8, 128), F32), V((192, 128), F32), V((2, 16, 128), F32), V((2, 16, 128), F32), V((48, 128), F32),
            V((40, 256), jnp.int32), V((8, 256), jnp.int32), pltpu.SMEM((8, 256), jnp.int32),
            V((16, 16, 128), BF16), V((16, 16, 128), BF16),
            V((4, 4, 16, 1536), BF16), V((16, 16, 1536), BF16), V((16, 1536), F32), V((4, 16, 384), BF16), V((4, 16, 384), BF16),
            V((4, 2, 4, 16, 1024), F32), V((4, 2, 4, 16, 512), BF16), V((2, 4, 2, 4, 16, 128), F32), V((16, 1536), BF16),
            V((4, 16, 384), BF16), V((4, 16, 384), BF16),
            DMA((6,)), DMA((3, 12)), DMA((3, 12)), DMA((3, 4)), DMA((3, 4)), DMA((3, 12)), DMA((3, 12)), DMA((3, 12)), DMA((3, 12)),
            DMA((3,)), DMA((3,)), DMA((3,)), DMA((3,)), DMA((3,)), DMA((3,)), DMA((16,)), DMA((16,)), DMA((16,)), DMA((16,)),
            DMA((3, 12)), DMA((3, 12)), DMA((3, 4)), DMA((3, 4)), DMA((3, 12)), DMA((3, 12)), DMA((3,)), DMA((3,)), DMA((3,)), DMA((3,)),
        ],
        compiler_params=pltpu.CompilerParams(collective_id=0, has_side_effects=True, vmem_limit_bytes=63 * 2**20),
    )(block_table.T, cached_len, expert_ids, expert_gates, queries, new_kv, hidden_in, norm_gain.reshape(48, 128),
      kv_pool, w_out, w_gate, w_up, w_down)


def solution(mesh):
    both = ("row", "col")
    return jax.shard_map(
        on_device,
        mesh=mesh,
        in_specs=(P(both, None, None), P(both, None, None), P(both, None, None), P(both, None, None), P(), P(), P("col", None),
                  P(), P(both, None, None), P(both, None, None), P("row", None, "col"), P("row", None, "col"), P("row", "col", None)),
        out_specs=P(both, None, None),
        check_vma=False,
    )
```

time: 195 us -> 156 us (0.80)
  Pallas kernels: 179 us -> 155 us
  local copies, waits for them, and re-layouts: 9.25 us -> 1.45 us
  other arithmetic: 6.19 us -> 0 us
    pallas_call x2 -> x1, Pallas kernels: 179 us -> 155 us  [on_device(): pl.pallas_call(layer_kernel, out_shape=jax.ShapeDtypeStruct((2, 2, 6144),...]
    reshape x9 -> x0, local copies, waits for them, and re-layouts: 5.87 us -> none  [the longest x2 1.46 us: on_device(): queries.reshape(2, 2, 3, 16, 128)]
where the time goes in v2:
time: 156 us
  Pallas kernels  155 us (99%)
    pallas_call x1, Pallas kernels, on_device(): pl.pallas_call(layer_kernel, out_shape=jax.ShapeDtypeStruct((2, 2, 6144),...  155 us

profile of v2, /device:TPU:0, one launch (start us, length us, event | category | flops | bytes accessed | tf_op | source)
XLA Modules:
  0.0 156.1 jit_solution(14531496038565772332)
XLA Ops:
  0.0 154.6 %shard_map.127 = bf16[2,2,6144]{2,1,0:T(2,128)(2,1)} custom-call(s32[64,256]{1,0:T(8,128)} %bitcast.2, s32[256]{0:T(256)} %clen.1, s32[2,2,2]{2,1,0:T(2,128)} %ids.1, f32[2,2,2]{2,1,0:T(2,128)} %gates.1, bf16[2,2,6144]{2,1,0:T(2,128)(2,1)} %queries.1, bf16[2,2,2048]{2,1,0:T(2,128)(2,1)} %new_kv.1, bf16[2,2,6144]{2,1,0:T(2,128)(2,1)} %hidden.1, ...), custom_call_target="tpu_custom_call" | custom-call | tf_op jit(solution)/shard_map/pallas_call | solution.py:722
  154.6 1.5 copy.15

commit v3 on v2

--- a/solution.py
+++ b/solution.py
@@ -12,13 +12,17 @@
 
 def where_am_i():
     r, c = lax.axis_index("row"), lax.axis_index("col")
-    return {"y": r // 2, "k": r % 2, "x": c // 4, "z": c % 4}
+    return {"y": lax.div(r, 2), "k": lax.rem(r, 2), "x": lax.div(c, 4), "z": lax.rem(c, 4)}
+
+
+def turned(v, step):
+    return lax.rem(v + (step + 4), 4)
 
 
 def device(me, **moved):
     at = dict(me)
     for name, step in moved.items():
-        at[name] = (me[name] + step) % (2 if name == "k" else 4)
+        at[name] = lax.rem(me[name] + step, 2) if name == "k" else turned(me[name], step)
     return (at["y"] * 2 + at["k"], at["x"] * 4 + at["z"])
 
 
@@ -54,7 +58,7 @@
 
 
 def shift(me, **moved):
-    return {n: (me[n] - s) % 4 for n, s in moved.items()}
+    return {n: turned(me[n], -s) for n, s in moved.items()}
 
 
 HALF = (slice(0, 2), slice(2, 4))
@@ -90,14 +94,14 @@
         hooks[0]()
     for p, (a, b, c) in enumerate(ORDERS):
         for d in (1, 3, 2):
-            landed(p, {a: (me[a] - d) % 4, b: me[b], c: me[c]}, d - 1)
+            landed(p, {a: turned(me[a], -d), b: me[b], c: me[c]}, d - 1)
         for d in (2, 1, 3):
             go(p, {b: me[b], c: me[c]}, {b: d}, 3 + d - 1)
     if hooks:
         hooks[1]()
     for p, (a, b, c) in enumerate(ORDERS):
         for d in (1, 3, 2):
-            landed(p, {b: (me[b] - d) % 4, c: me[c]}, 3 + d - 1)
+            landed(p, {b: turned(me[b], -d), c: me[c]}, 3 + d - 1)
         go(p, {b: HALF[0], c: me[c]}, {c: 1}, 6)
         go(p, {b: HALF[1], c: me[c]}, {c: -1}, 9)
         go(p, {b: HALF[1], c: me[c]}, {c: 1}, 7)
@@ -108,27 +112,27 @@
 
     def both_cores(i, d):
         for p, (a, b, c) in enumerate(ORDERS):
-            across(p, {c: (me[c] + d) % 4}, i, 1 - k).wait_recv()
+            across(p, {c: turned(me[c], d)}, i, 1 - k).wait_recv()
         if on_line:
             on_line(d)
 
-    for p, (a, b, c) in enumerate(ORDERS):
-        landed(p, {b: HALF[0], c: (me[c] - 1) % 4}, 6)
-        go(p, {b: HALF[0], c: (me[c] - 1) % 4}, {c: 1}, 10)
-        landed(p, {b: HALF[1], c: (me[c] + 1) % 4}, 9)
-        go(p, {b: HALF[1], c: (me[c] + 1) % 4}, {c: -1}, 11)
     both_cores(0, 0)
     for p, (a, b, c) in enumerate(ORDERS):
-        landed(p, {b: HALF[1], c: (me[c] - 1) % 4}, 7)
-        cross(p, {c: (me[c] - 1) % 4}, 1)
-        landed(p, {b: HALF[0], c: (me[c] + 1) % 4}, 8)
-        cross(p, {c: (me[c] + 1) % 4}, 2)
+        landed(p, {b: HALF[0], c: turned(me[c], -1)}, 6)
+        go(p, {b: HALF[0], c: turned(me[c], -1)}, {c: 1}, 10)
+        landed(p, {b: HALF[1], c: turned(me[c], 1)}, 9)
+        go(p, {b: HALF[1], c: turned(me[c], 1)}, {c: -1}, 11)
+    for p, (a, b, c) in enumerate(ORDERS):
+        landed(p, {b: HALF[1], c: turned(me[c], -1)}, 7)
+        cross(p, {c: turned(me[c], -1)}, 1)
+        landed(p, {b: HALF[0], c: turned(me[c], 1)}, 8)
+        cross(p, {c: turned(me[c], 1)}, 2)
     both_cores(1, 3)
     both_cores(2, 1)
     for p, (a, b, c) in enumerate(ORDERS):
-        landed(p, {b: HALF[0], c: (me[c] + 2) % 4}, 10)
-        landed(p, {b: HALF[1], c: (me[c] + 2) % 4}, 11)
-        cross(p, {c: (me[c] + 2) % 4}, 3)
+        landed(p, {b: HALF[0], c: turned(me[c], 2)}, 10)
+        landed(p, {b: HALF[1], c: turned(me[c], 2)}, 11)
+        cross(p, {c: turned(me[c], 2)}, 3)
     both_cores(3, 2)
     for copy in started:
         copy.wait_send()
@@ -164,7 +168,7 @@
     def add(p, b, c, at, half, terms):
         rest = rest_of(c)
 
-        def body(n, _):
+        for n in range(8):
             i_b, i_a = 2 * half + n // 4, n % 4
             idx = {c: at, **{m: (i_b if m == b else i_a) for m in rest}}
             mine = (idx["y"], k, idx["x"], idx["z"]) + parts[p]
@@ -172,19 +176,16 @@
             for t in terms:
                 total += t(idx, rest, n).astype(F32)
             buf[mine] = total.astype(BF16)
-            return 0
-
-        lax.fori_loop(0, 8, body, 0, unroll=4)
 
     for p, (a, b, c) in enumerate(ORDERS):
         ready(p)
-        far, right, left = (me[c] + 2) % 4, (me[c] + 1) % 4, (me[c] - 1) % 4
+        far, right, left = turned(me[c], 2), turned(me[c], 1), turned(me[c], -1)
         go(p, {c: far, b: HALF[0]}, {c: 1}, fwd_dst(fwd, p, 0, a, b, c), 0)
         go(p, {c: far, b: HALF[1]}, {c: -1}, fwd_dst(fwd, p, 1, a, b, c), 1)
         go(p, {c: right, b: HALF[1]}, {c: 1}, sub(line, p, 0, b, c, 1), 2)
         go(p, {c: left, b: HALF[0]}, {c: -1}, sub(line, p, 1, b, c, 0), 3)
     for p, (a, b, c) in enumerate(ORDERS):
-        right, left = (me[c] + 1) % 4, (me[c] - 1) % 4
+        right, left = turned(me[c], 1), turned(me[c], -1)
         landed(p, fwd_dst(fwd, p, 0, a, b, c), 0)
         add(p, b, c, right, 0, [fwd_at(fwd, p, 0, a, b, c)])
         go(p, {c: right, b: HALF[0]}, {c: 1}, sub(line, p, 0, b, c, 0), 4)
@@ -199,7 +200,7 @@
         for h in range(2):
             add(p, b, c, me[c], h, [lt(0), lt(1)])
         for d in (2, 1, 3):
-            go(p, {c: me[c], b: (me[b] + d) % 4}, {b: d}, r2.at[p, d - 1], 5 + d)
+            go(p, {c: me[c], b: turned(me[b], d)}, {b: d}, r2.at[p, d - 1], 5 + d)
     for p, (a, b, c) in enumerate(ORDERS):
         for d in (1, 2, 3):
             landed(p, r2.at[p, d - 1], 5 + d)
@@ -211,7 +212,7 @@
                 total += r2[p, d, i].astype(F32)
             buf[mine] = total.astype(BF16)
         for d in (2, 1, 3):
-            go(p, {c: me[c], b: me[b], a: (me[a] + d) % 4}, {a: d}, r3.at[p, d - 1], 8 + d)
+            go(p, {c: me[c], b: me[b], a: turned(me[a], d)}, {a: d}, r3.at[p, d - 1], 8 + d)
     sums = []
     for p, (a, b, c) in enumerate(ORDERS):
         for d in (1, 2, 3):
@@ -245,7 +246,7 @@
 
 
 def layer_kernel(table, clen, ids, gates, queries, new_kv, hidden, gain, kv_h, wo_h, wg_h, wu_h, wd_h, o_ref,
-                 X, A, KV, VT, WO, WG, WU, WD, accs, ms, ls, Z, Zm, Zl, St, Cst, core, fa, fb, line, r2, r3, sf, sl, St2, s2, St3, s3, Wt,
+                 X, A, KV, VT, WO, WG, WU, WD, accs, ms, ls, ms2, ls2, Z, Zm, Zl, PI, PM, St, Cst, core, fa, fb, line, r2, r3, sf, sl, St2, s2, St3, s3,
                  U, NK, NV, GF, CC, info_v, info, G, H, O, Rv, hid, hin, hrec, acc, act, scal, resid, fout, fin,
                  lsem, gs, gr, gcs, gcr, ss_, sr, ts, tr, scs, scr, tcs, tcr, hs, hr, as_, ar, ps, pr,
                  gs2, gr2, gcs2, gcr2, ss2, sr2, scs2, scr2, fs, fr):
@@ -284,6 +285,7 @@
         found = jnp.where((r == 32) | (r == 33), (rank * 2 + r - 32) * 64, found)
         owner = jnp.where(found >= 0, found // 64, -1)
         as_row = lambda v: jnp.max(jnp.where(r == c, v, -1), axis=0, keepdims=True)
+        PI[...] = jnp.where(r == 35, 1, jnp.where(owner < 0, 0, owner % 2))
         owner_row, place_row = as_row(owner), as_row(jnp.where(found >= 0, found % 64, 0))
         before = jnp.max(jnp.where((owner == owner_row) & (r < c) & (owner >= 0), r, -1), axis=0, keepdims=True)
         info_v[1:2, 0:128] = jnp.where(before < 0, EMPTY, before)
@@ -308,7 +310,7 @@
         for z in range(4):
             hin[z] = jnp.concatenate([f[:, 1536 * z + 384 * q : 1536 * z + 384 * q + 384] for q in range(4)], axis=0).astype(BF16)
         for d in (1, 2, 3):
-            c = remote(hin.at[(me["z"] + d) % 4], hrec.at[me["z"]], hs.at[d - 1], hr.at[d - 1], device(me, z=d))
+            c = remote(hin.at[turned(me["z"], d)], hrec.at[me["z"]], hs.at[d - 1], hr.at[d - 1], device(me, z=d))
             c.start()
             started.append(c)
         hrec[me["z"]] = hin[me["z"]]
@@ -324,86 +326,124 @@
         lax.fori_loop(0, 32, turn, 0, unroll=4)
         fresh_slots()
 
-    lane = lax.broadcasted_iota(jnp.int32, (128, 192), 1)
-    rowi = lax.broadcasted_iota(jnp.int32, (128, 192), 0)
-    head_kv = ((lane // 64) * 16 + lane % 16) // 6
-    lane_i = (lane // 32) % 2
+    lane = lax.broadcasted_iota(jnp.int32, (128, 128), 1)
+    rowi = lax.broadcasted_iota(jnp.int32, (128, 128), 0)
+    head_kv = jnp.where(lane < 96, ((lane // 32) * 16 + lane % 16) // 6, -1)
     lane_s = (lane // 16) % 2
     same = jnp.where(head_kv == rowi // 16, rowi % 16, 99)
+    to_bits = 128 ** -0.5 * 1.4426950408889634
+
+    def query_rows(at, i):
+        first = jnp.broadcast_to(jnp.asarray(i, jnp.int32), (32, 128)) == 0
+        pieces = []
+        for p in (0, 1, 2):
+            a, b = (X[at + (slice(64 * p + o, 64 * p + o + 32), slice(None))].astype(F32) for o in (0, 32))
+            pieces.append(jnp.where(first, a, b).astype(BF16))
+        return jnp.concatenate(pieces + pieces[:1], axis=0)
+
+    def attend(st, ok, vt, j):
+        st = jnp.where(ok, st, -1e30)
+        m = jnp.max(st, axis=0, keepdims=True)
+        w = jnp.exp2((st - m) * to_bits)
+        accs[j] = jnp.dot(vt, w.astype(BF16), preferred_element_type=F32)
+        ms[j] = m * to_bits
+        ls[j] = jnp.sum(w, axis=0, keepdims=True)
 
     def fresh_slots():
-        own = X[me["y"], k, me["x"], me["z"], 0:192, :]
+        r = rowi[:16]
+        for i in range(32, 36):
+            ms[i] = jnp.full((1, 128), -1e30, F32)
+            ls[i] = jnp.zeros((1, 128), F32)
+        ms2[32:40, :] = jnp.full((8, 128), -1e30, F32)
+        ls2[32:40, :] = jnp.zeros((8, 128), F32)
+        row2 = lax.broadcasted_iota(jnp.int32, (256, 384), 0)
+        col2 = lax.broadcasted_iota(jnp.int32, (256, 384), 1)
+        source = (col2 % 128) // 64 * 128 + col2 // 128 * 32 + col2 % 32
         for i in range(2):
-            st = lax.dot_general(NK[i].astype(BF16), own, (((1,), (1,)), ((), ())), preferred_element_type=F32) * (128 ** -0.5)
-            r = rowi[:16]
-            ok = (head_kv[:16] == r // 2) & (r % 2 <= lane_s[:16]) & (lane_i[:16] == i)
-            st = jnp.where(ok, st, -1e30)
-            m = jnp.max(st, axis=0, keepdims=True)
-            w = jnp.exp(st - m)
-            accs[32 + i] = jnp.dot(NV[i].T.astype(BF16), w.astype(BF16), preferred_element_type=F32)
-            ms[32 + i] = m
-            ls[32 + i] = jnp.sum(w, axis=0, keepdims=True)
-            accs[EMPTY + i] = jnp.zeros((128, 192), F32)
-            ms[EMPTY + i] = jnp.full((1, 192), -1e30, F32)
-            ls[EMPTY + i] = jnp.zeros((1, 192), F32)
+            PM[i] = jnp.where((row2 == source) & ((col2 // 32) % 2 == i), 1.0, 0.0).astype(BF16)
+            own = query_rows((me["y"], k, me["x"], me["z"]), i)
+            st = lax.dot_general(NK[i].astype(BF16), own, (((1,), (1,)), ((), ())), preferred_element_type=F32)
+            attend(st, (head_kv[:16] == r // 2) & (r % 2 <= lane_s[:16]), NV[i].T.astype(BF16), 32 + i)
+            accs[EMPTY + i] = jnp.zeros((128, 128), F32)
 
     gather_blocks(X, me, QPARTS, gs, gr, gcs, gcr, (find_blocks, small_things, turn_values))
     info_load.wait()
 
-    def slot(j, _):
+    def score(j, _):
         rq = info[2, j]
-        seen = jnp.clip(clen[rq] - 16 * info[3, j], 0, 16)
-        q = X[rq // 64, (rq // 32) % 2, (rq // 8) % 4, (rq // 2) % 4, 0:192, :]
+        q = query_rows((lax.div(rq, 64), lax.rem(lax.div(rq, 32), 2), lax.rem(lax.div(rq, 8), 4), lax.rem(lax.div(rq, 2), 4)), lax.rem(rq, 2))
         ks = jnp.concatenate([KV[j, :, 128 * g : 128 * g + 128] for g in range(8)], axis=0)
-        st = lax.dot_general(ks, q, (((1,), (1,)), ((), ())), preferred_element_type=F32) * (128 ** -0.5)
-        st = jnp.where((same < seen) & (lane_i == rq % 2), st, -1e30)
+        accs[j] = lax.dot_general(ks, q, (((1,), (1,)), ((), ())), preferred_element_type=F32)
+        return 0
+
+    def weigh(j, _):
+        seen = jnp.clip(clen[info[2, j]] - 16 * info[3, j], 0, 16)
+        st = jnp.where(same < seen, accs[j], -1e30)
         m = jnp.max(st, axis=0, keepdims=True)
-        w = jnp.exp(st - m)
-        accs[j] = jnp.dot(VT[j], w.astype(BF16), preferred_element_type=F32)
-        ms[j] = m
+        w = jnp.exp2((st - m) * to_bits)
+        ms[j] = m * to_bits
         ls[j] = jnp.sum(w, axis=0, keepdims=True)
+        Z[j, 0] = w[:64].astype(BF16)
+        Z[j, 1] = w[64:].astype(BF16)
         return 0
 
-    lax.fori_loop(0, 32, slot, 0, unroll=4)
+    def mix(j, _):
+        accs[j] = jnp.dot(VT[j], jnp.concatenate([Z[j, 0], Z[j, 1]], axis=0), preferred_element_type=F32)
+        return 0
+
+    lax.fori_loop(0, 32, score, 0, unroll=8)
+    lax.fori_loop(0, 32, weigh, 0, unroll=4)
+    lax.fori_loop(0, 32, mix, 0, unroll=8)
     def chain(j, _):
         pj = info[1, j]
-        i = info[2, j] % 2
         m0, m1 = ms[j], ms[pj]
         m = jnp.maximum(m0, m1)
-        w0, w1 = jnp.exp(m0 - m), jnp.exp(m1 - m)
-        acc = accs[j] * w0 + accs[pj] * w1
+        w0, w1 = jnp.exp2(m0 - m), jnp.exp2(m1 - m)
         l = ls[j] * w0 + ls[pj] * w1
-        accs[j] = acc
+        accs[j] = accs[j] * w0 + accs[pj] * w1
+        ls[j] = l
         ms[j] = m
-        ls[j] = l
-        mine = lane_i == i
-        acc = jnp.where(mine, acc, 0.0)
-        m = jnp.where(mine[:1], m, 0.0)
-        l = jnp.where(mine[:1], l, 0.0)
+        ms2[pl.ds(j, 1), :] = m
+        ls2[pl.ds(j, 1), :] = l
+        return 0
+
+    def put(j, _):
+        both = jnp.concatenate([accs[j, 0:64, :], accs[j, 64:128, :]], axis=1).astype(BF16)
+        t = jnp.dot(both, PM[lax.rem(info[2, j], 2)], preferred_element_type=F32).astype(BF16)
         for p in range(3):
-            s = slice(64 * p, 64 * p + 64)
-            Z[j, p] = jnp.concatenate([acc[:64, s], acc[64:, s]], axis=1).astype(BF16)
-            Zm[j, p] = jnp.concatenate([m[:, s], m[:, s]], axis=1)
-            Zl[j, p] = jnp.concatenate([l[:, s], l[:, s]], axis=1)
+            Z[j, p] = t[:, 128 * p : 128 * p + 128]
         return 0
 
-    lax.fori_loop(0, 36, chain, 0, unroll=2)
-
+    lax.fori_loop(0, 34, chain, 0, unroll=2)
+    lax.fori_loop(0, 36, put, 0, unroll=6)
+    ln = lane[:40]
+    for v, Zv in ((ms2, Zm), (ls2, Zl)):
+        for p in range(3):
+            t = jnp.where(ln < 64, pltpu.roll(v[...], (128 - 32 * p) % 128, 1), pltpu.roll(v[...], (192 - 32 * p) % 128, 1))
+            t = jnp.where(ln % 64 < 32, t, 0.0)
+            t = jnp.where(PI[...] == 0, t, pltpu.roll(t, 32, 1))
+            for j in range(36):
+                Zv[p, j] = t[j : j + 1]
     def spread(kk, ps_):
-        def body(n, _):
-            y, x, z = n // 16, (n // 4) % 4, n % 4
-            to = y * 32 + kk * 16 + x * 4 + z
-            s0, s1_ = info[0, 2 * to], info[0, 2 * to + 1]
-            at = {"y": y, "x": x, "z": z}
-            for p in ps_:
-                a, b, c = ORDERS[p]
-                A[y, kk, x, z, 64 * p : 64 * p + 64, :] = Z[s0, p] + Z[s1_, p]
-                row = pl.ds((at[b] % 2) * 4 + at[a], 1)
-                St[p, kk, at[c], at[b] // 2, 0, row, :] = Zm[s0, p] + Zm[s1_, p]
-                St[p, kk, at[c], at[b] // 2, 1, row, :] = Zl[s0, p] + Zl[s1_, p]
+        def body(y, _):
+            for x in range(4):
+                for z in range(4):
+                    to = y * 32 + kk * 16 + x * 4 + z
+                    s0, s1_ = info[0, 2 * to], info[0, 2 * to + 1]
+                    for p in ps_:
+                        A[y, kk, x, z, 64 * p : 64 * p + 64, :] = Z[s0, p] + Z[s1_, p]
+                        m, l = (Zv[p, s0] + Zv[p, s1_] for Zv in (Zm, Zl))
+                        if p == 0:
+                            at = (z, lax.div(y, 2), pl.ds(lax.rem(y, 2) * 4 + x, 1))
+                        elif p == 1:
+                            at = (x, z // 2, pl.ds((z % 2) * 4 + y, 1))
+                        else:
+                            at = (y, x // 2, slice((x % 2) * 4 + z, (x % 2) * 4 + z + 1))
+                        St[(p, kk) + at[:2] + (0, at[2], slice(None))] = m
+                        St[(p, kk) + at[:2] + (1, at[2], slice(None))] = l
             return 0
 
-        lax.fori_loop(0, 64, body, 0, unroll=4)
+        lax.fori_loop(0, 4, body, 0)
 
     cores = []
     for p in range(3):
@@ -428,7 +468,7 @@
 
     def merge(stats):
         top = functools.reduce(jnp.maximum, [m for m, _ in stats])
-        ws = [jnp.exp(m - top) for m, _ in stats]
+        ws = [jnp.exp2(m - top) for m, _ in stats]
         return top, sum(w * l for w, (_, l) in zip(ws, stats)), ws
 
     def others(c):
@@ -446,20 +486,13 @@
         top, tot, ws = merge(stats)
         St[p, k, at, h, 0] = top
         St[p, k, at, h, 1] = tot
-        for i, w in enumerate(ws):
-            Wt[i] = w
-
-        def body(n, _):
+        for n in range(8):
             idx = {c: at, b: 2 * h + n // 4, a: n % 4}
-            row = pl.ds(n, 1)
             mine = (idx["y"], k, idx["x"], idx["z"]) + QPARTS[p]
-            t = A[mine].astype(F32) * Wt[0, row, :]
+            t = A[mine].astype(F32) * ws[0][n : n + 1]
             for i, (block, _) in enumerate(sources):
-                t += block(idx, n).astype(F32) * Wt[i + 1, row, :]
+                t += block(idx, n).astype(F32) * ws[i + 1][n : n + 1]
             A[mine] = t.astype(BF16)
-            return 0
-
-        lax.fori_loop(0, 8, body, 0, unroll=4)
 
     def from_core(p, at, h):
         return (lambda idx, n: core[(idx["y"], idx["x"], idx["z"]) + QPARTS[p]]), Cst[p, at, h]
@@ -476,7 +509,7 @@
     for p, (a, b, c) in enumerate(ORDERS):
         for copy in cores[p]:
             copy.wait_recv()
-        far, right, left = (me[c] + 2) % 4, (me[c] + 1) % 4, (me[c] - 1) % 4
+        far, right, left = turned(me[c], 2), turned(me[c], 1), turned(me[c], -1)
         blend(p, far, 0, [from_core(p, far, 0)])
         go(p, {c: far, b: HALF[0]}, {c: 1}, fwd_dst(fwd, p, 0, a, b, c), 0, St.at[p, k, far, 0], sf.at[p, 0])
         blend(p, far, 1, [from_core(p, far, 1)])
@@ -486,7 +519,7 @@
         blend(p, left, 0, [from_core(p, left, 0)])
         go(p, {c: left, b: HALF[0]}, {c: -1}, half_line(p, 1, b, c, 0), 3, St.at[p, k, left, 0], sl.at[p, 1, 0])
     for p, (a, b, c) in enumerate(ORDERS):
-        right, left = (me[c] + 1) % 4, (me[c] - 1) % 4
+        right, left = turned(me[c], 1), turned(me[c], -1)
         landed(p, fwd_dst(fwd, p, 0, a, b, c), 0, sf.at[p, 0])
         blend(p, right, 0, [from_core(p, right, 0), from_fwd(p, 0)])
         go(p, {c: right, b: HALF[0]}, {c: 1}, half_line(p, 0, b, c, 0), 4, St.at[p, k, right, 0], sl.at[p, 0, 0])
@@ -505,7 +538,7 @@
                 St2[p, 2 * h + i, 0:4] = St[p, k, me[c], h, 0, 4 * i : 4 * i + 4]
                 St2[p, 2 * h + i, 4:8] = St[p, k, me[c], h, 1, 4 * i : 4 * i + 4]
         for d in (2, 1, 3):
-            at = (me[b] + d) % 4
+            at = turned(me[b], d)
             go(p, {c: me[c], b: at}, {b: d}, r2.at[p, d - 1], 5 + d, St2.at[p, at], s2.at[p, d - 1])
     for p, (a, b, c) in enumerate(ORDERS):
         for d in (1, 2, 3):
@@ -522,7 +555,7 @@
             St3[p, i, 0:1] = top[i : i + 1]
             St3[p, i, 1:2] = tot[i : i + 1]
         for d in (2, 1, 3):
-            at = (me[a] + d) % 4
+            at = turned(me[a], d)
             go(p, {c: me[c], b: me[b], a: at}, {a: d}, r3.at[p, d - 1], 8 + d, St3.at[p, at], s3.at[p, d - 1])
     for p, (a, b, c) in enumerate(ORDERS):
         for d in (1, 2, 3):
@@ -545,7 +578,7 @@
     steps = [(dx, dz) for dz in (2, 1, 3, 0) for dx in (2, 1, 3, 0) if dx or dz]
 
     def peer(dx, dz):
-        return ((me["x"] + dx) % 4) * 4 + (me["z"] + dz) % 4
+        return (turned(me["x"], dx)) * 4 + turned(me["z"], dz)
 
     for dx, dz in steps:
         c = remote(G.at[peer(dx, dz)], H.at[col], as_.at[dx * 4 + dz], ar.at[dx * 4 + dz], device(me, x=dx, z=dz))
@@ -553,7 +586,7 @@
         started.append(c)
     H[col] = G[col]
     for d in (1, 2, 3):
-        there = hrec.at[(me["z"] - d) % 4]
+        there = hrec.at[turned(me["z"], -d)]
         remote(there, there, hs.at[d - 1], hr.at[d - 1], device(me, k=1)).wait_recv()
     for z in range(4):
         f = hrec[z].astype(F32)
@@ -568,13 +601,13 @@
         heads.append(jnp.concatenate([hf[c][4 * hh : 4 * hh + 4] for c in range(16)], axis=0).astype(BF16))
     lhs = jnp.concatenate(heads, axis=1)
     for dz in (2, 1, 3, 0):
-        zz = (me["z"] + dz) % 4
+        zz = turned(me["z"], dz)
         res = jnp.dot(lhs, WO[:, pl.ds(pl.multiple_of(zz * 1536, 1536), 1536)], preferred_element_type=F32).astype(BF16)
         for x in range(4):
             O[x, zz] = res[16 * x : 16 * x + 16]
         for dx in (2, 1, 3, 0):
             if dx or dz:
-                c = remote(O.at[(me["x"] + dx) % 4, zz], Rv.at[col], ps.at[dx * 4 + dz], pr.at[dx * 4 + dz], device(me, x=dx, z=dz))
+                c = remote(O.at[turned(me["x"], dx), zz], Rv.at[col], ps.at[dx * 4 + dz], pr.at[dx * 4 + dz], device(me, x=dx, z=dz))
                 c.start()
                 started.append(c)
     Rv[col] = O[me["x"], me["z"]]
@@ -619,15 +652,16 @@
     expert = me["y"] * 2 + k
     acc[...] = jnp.zeros_like(acc)
 
-    def add_product(at, rows, k0):
-        x = jnp.concatenate([X[rows + (slice(16 * n, 16 * n + 16), slice(None))] for n in range(4 * k0[1], 4 * k0[1] + 4)], axis=-1)
-        lead = x.shape[:-1]
-        x = x.reshape(-1, 512)
-        depth = pl.ds(pl.multiple_of(k0[0] * 1536 + 512 * k0[1], 512), 512)
+    def add_products(at, terms):
+        xs = []
+        for rows, z, p in terms:
+            x = jnp.concatenate([X[rows + (slice(16 * n, 16 * n + 16), slice(None))] for n in range(4 * p, 4 * p + 4)], axis=-1)
+            lead = x.shape[:-1]
+            xs.append((x.reshape(-1, 512), pl.ds(pl.multiple_of(z * 1536 + 512 * p, 512), 512)))
         for n, W in enumerate((WG, WU)):
             for h in range(2):
                 cols = slice(512 * n + 256 * h, 512 * n + 256 * h + 256)
-                r = jnp.dot(x, W[depth, 256 * h : 256 * h + 256], preferred_element_type=F32)
+                r = sum(jnp.dot(x, W[depth, 256 * h : 256 * h + 256], preferred_element_type=F32) for x, depth in xs)
                 acc[at + (cols,)] += r.reshape(lead + (256,))
 
     def on_line(d):
@@ -635,15 +669,10 @@
             loads[0].wait()
             loads[1].wait()
         full = slice(None)
-        z, x, y = (me["z"] + d) % 4, (me["x"] + d) % 4, (me["y"] + d) % 4
-        add_product((full, full, full, full), (full, full, full, z), (z, 0))
-
-        def body(zz, _):
-            add_product((full, full, x, full), (full, full, x, zz), (zz, 1))
-            add_product((y, full, full, full), (y, full, full, zz), (zz, 2))
-            return 0
-
-        lax.fori_loop(0, 4, body, 0)
+        z, x, y = turned(me["z"], d), turned(me["x"], d), turned(me["y"], d)
+        add_products((full, full, full, full), [((full, full, full, z), z, 0)])
+        add_products((full, full, x, full), [((full, full, x, zz), zz, 1) for zz in range(4)])
+        add_products((y, full, full, full), [((y, full, full, zz), zz, 2) for zz in range(4)])
 
     gather_blocks(X, me, XPARTS, gs, gr, gcs, gcr, (), on_line)
     loads[2].wait()
@@ -656,9 +685,10 @@
     scal[0] = jnp.broadcast_to(lax.rsqrt(squares * (1.0 / 6144.0) + 1e-5), (512, 128)).reshape(4, 2, 4, 16, 128)
     scal[1] = jnp.broadcast_to(weight, (512, 128)).reshape(4, 2, 4, 16, 128)
     started = []
-    for kk in (1 - k, k):
+
+    def activate(kk):
+        at = (slice(None), kk, slice(None), slice(None))
         for n in range(4):
-            at = (slice(None), kk, slice(None), slice(None))
             rs = scal[(0,) + at].reshape(256, 128)
             g = acc[at + (slice(128 * n, 128 * n + 128),)].reshape(256, 128) * rs
             u = acc[at + (slice(512 + 128 * n, 640 + 128 * n),)].reshape(256, 128) * rs
@@ -679,9 +709,11 @@
 
         lax.fori_loop(0, 4, body, 0)
 
+    activate(1 - k)
     for p in range(3):
         down(1 - k, p, False)
         started.append(send_core(A, me, QPARTS, core, scs, scr, p))
+    activate(k)
 
     def ready(p):
         started[p].wait_recv()
@@ -694,12 +726,12 @@
         fout[z] = jnp.concatenate([rows[:, 384 * q : 384 * q + 384] for q in range(4)], axis=0).astype(BF16)
     outs = []
     for d in (2, 1, 3):
-        c = remote(fout.at[(me["z"] + d) % 4], fin.at[me["z"]], fs.at[d - 1], fr.at[d - 1], device(me, z=d))
+        c = remote(fout.at[turned(me["z"], d)], fin.at[me["z"]], fs.at[d - 1], fr.at[d - 1], device(me, z=d))
         c.start()
         outs.append(c)
     fin[me["z"]] = fout[me["z"]]
     for d in (1, 3, 2):
-        there = fin.at[(me["z"] - d) % 4]
+        there = fin.at[turned(me["z"], -d)]
         remote(there, there, fs.at[d - 1], fr.at[d - 1], device(me, k=1)).wait_recv()
     for c in outs:
         c.wait_send()
@@ -727,13 +759,13 @@
         scratch_shapes=[
             V((4, 2, 4, 4, 208, 128), BF16), V((4, 2, 4, 4, 192, 128), BF16), V((32, 16, 2048), BF16), V((32, 128, 128), BF16),
             V((384, 6144), BF16), V((6144, 512), BF16), V((6144, 512), BF16), V((512, 6144), BF16),
-            V((36, 128, 192), F32), V((36, 1, 192), F32), V((36, 1, 192), F32),
-            V((36, 3, 64, 128), BF16), V((36, 3, 1, 128), F32), V((36, 3, 1, 128), F32),
+            V((36, 128, 128), F32), V((36, 1, 128), F32), V((36, 1, 128), F32), V((40, 128), F32), V((40, 128), F32),
+            V((36, 3, 64, 128), BF16), V((3, 36, 1, 128), F32), V((3, 36, 1, 128), F32), V((40, 128), jnp.int32), V((2, 256, 384), BF16),
             V((3, 2, 4, 2, 2, 8, 128), F32), V((3, 4, 2, 2, 8, 128), F32), V((4, 4, 4, 192, 128), BF16),
             V((3, 2, 2, 4, 64, 128), BF16), V((3, 2, 4, 2, 64, 128), BF16), V((3, 2, 4, 4, 64, 128), BF16),
             V((3, 3, 4, 64, 128), BF16), V((3, 3, 64, 128), BF16),
             V((3, 2, 2, 8, 128), F32), V((3, 2, 2, 2, 8, 128), F32), V((3, 4, 8, 128), F32), V((3, 3, 8, 128), F32), V((3, 4, 8, 128), F32), V((3, 3, 8, 128), F32),
-            V((4, 8, 128), F32), V((192, 128), F32), V((2, 16, 128), F32), V((2, 16, 128), F32), V((48, 128), F32),
+            V((192, 128), F32), V((2, 16, 128), F32), V((2, 16, 128), F32), V((48, 128), F32),
             V((40, 256), jnp.int32), V((8, 256), jnp.int32), pltpu.SMEM((8, 256), jnp.int32),
             V((16, 16, 128), BF16), V((16, 16, 128), BF16),
             V((4, 4, 16, 1536), BF16), V((16, 16, 1536), BF16), V((16, 1536), F32), V((4, 16, 384), BF16), V((4, 16, 384), BF16),

time: 156 us -> 143 us (0.917)
  Pallas kernels: 155 us -> 141 us
    pallas_call x1, Pallas kernels: 155 us -> 141 us  [on_device(): pl.pallas_call(layer_kernel, out_shape=jax.ShapeDtypeStruct((2, 2, 6144),...]
where the time goes in v3:
time: 143 us; the launch traced here: 142 us
  Pallas kernels  141 us (99%)
  local copies, waits for them, and re-layouts  1.45 us (1%)
    pallas_call x1, Pallas kernels, on_device(): pl.pallas_call(layer_kernel, out_shape=jax.ShapeDtypeStruct((2, 2, 6144),...  141 us

profile of v3, /device:TPU:0, one launch (start us, length us, event | category | flops | bytes accessed | tf_op | source)
XLA Modules:
  0.0 142.3 jit_solution(9159711871564759260)
XLA Ops:
  0.0 140.8 %shard_map.127 = bf16[2,2,6144]{2,1,0:T(2,128)(2,1)} custom-call(s32[64,256]{1,0:T(8,128)} %bitcast.2, s32[256]{0:T(256)} %clen.1, s32[2,2,2]{2,1,0:T(2,128)} %ids.1, f32[2,2,2]{2,1,0:T(2,128)} %gates.1, bf16[2,2,6144]{2,1,0:T(2,128)(2,1)} %queries.1, bf16[2,2,2048]{2,1,0:T(2,128)(2,1)} %new_kv.1, bf16[2,2,6144]{2,1,0:T(2,128)(2,1)} %hidden.1, ...), custom_call_target="tpu_custom_call" | custom-call | tf_op jit(solution)/shard_map/pallas_call | solution.py:754
  140.8 1.5 %copy.15 = bf16[2,2,6144]{2,1,0:T(2,128)(2,1)} copy(bf16[2,2,6144]{2,1,0:T(2,128)(2,1)} %shard_map.127) | data formatting | bytes 98304

commit v4 on v3

--- a/solution.py
+++ b/solution.py
@@ -265,7 +265,7 @@
         q = queries[i].astype(F32)
         for h in range(48):
             U[pl.ds((h // 16) * 64 + i * 32 + h % 16, 2, stride=16), :] = q[:, 128 * h : 128 * h + 128]
-    X[me["y"], k, me["x"], me["z"], 0:192, :] = U[...].astype(BF16)
+    X[me["y"], k, me["x"], me["z"], 0:192, :] = U[0:192, :].astype(BF16)
     greet(me, plane=True)
     started = []
 
@@ -765,7 +765,7 @@
             V((3, 2, 2, 4, 64, 128), BF16), V((3, 2, 4, 2, 64, 128), BF16), V((3, 2, 4, 4, 64, 128), BF16),
             V((3, 3, 4, 64, 128), BF16), V((3, 3, 64, 128), BF16),
             V((3, 2, 2, 8, 128), F32), V((3, 2, 2, 2, 8, 128), F32), V((3, 4, 8, 128), F32), V((3, 3, 8, 128), F32), V((3, 4, 8, 128), F32), V((3, 3, 8, 128), F32),
-            V((192, 128), F32), V((2, 16, 128), F32), V((2, 16, 128), F32), V((48, 128), F32),
+            V((256, 128), F32), V((2, 16, 128), F32), V((2, 16, 128), F32), V((48, 128), F32),
             V((40, 256), jnp.int32), V((8, 256), jnp.int32), pltpu.SMEM((8, 256), jnp.int32),
             V((16, 16, 128), BF16), V((16, 16, 128), BF16),
             V((4, 4, 16, 1536), BF16), V((16, 16, 1536), BF16), V((16, 1536), F32), V((4, 16, 384), BF16), V((4, 16, 384), BF16),

time: 143 us -> 142 us (level)
  no operation moved by 1% of the time
where the time goes in v4:
time: 142 us
  Pallas kernels  140 us (99%)
  local copies, waits for them, and re-layouts  1.45 us (1%)
    pallas_call x1, Pallas kernels, on_device(): pl.pallas_call(layer_kernel, out_shape=jax.ShapeDtypeStruct((2, 2, 6144),...  140 us

profile of v4, /device:TPU:0, one launch (start us, length us, event | category | flops | bytes accessed | tf_op | source)
XLA Modules:
  0.0 141.8 jit_solution(238289756966819161)
XLA Ops:
  0.0 140.3 %shard_map.127 = bf16[2,2,6144]{2,1,0:T(2,128)(2,1)} custom-call(s32[64,256]{1,0:T(8,128)} %bitcast.2, s32[256]{0:T(256)} %clen.1, s32[2,2,2]{2,1,0:T(2,128)} %ids.1, f32[2,2,2]{2,1,0:T(2,128)} %gates.1, bf16[2,2,6144]{2,1,0:T(2,128)(2,1)} %queries.1, bf16[2,2,2048]{2,1,0:T(2,128)(2,1)} %new_kv.1, bf16[2,2,6144]{2,1,0:T(2,128)(2,1)} %hidden.1, ...), custom_call_target="tpu_custom_call" | custom-call | tf_op jit(solution)/shard_map/pallas_call | solution.py:754
  140.3 1.5 %copy.15 = bf16[2,2,6144]{2,1,0:T(2,128)(2,1)} copy(bf16[2,2,6144]{2,1,0:T(2,128)(2,1)} %shard_map.127) | data formatting | bytes 98304
